TPU v7x, 128 devices: a whole 4x4x4 slice. The times are simulated.
128 devices in a mesh: slab: 4 (over x), dom: 32 (over y, z, core).
Axes of the slice: x: 4, y: 4, z: 4, core: 2. Of those that a mesh axis runs over, the one named last changes fastest.
Arguments:
- incoming: float32 [4, 8192, 4, 128], P('slab', 'dom'), may hold values from -8 to 65, as said below
- dest: int32 [4, 8192], P('slab', 'dom'), may hold values from 0 to 8191, as said below
- counts: int32 [8, 64, 64], P('slab', 'dom'), may hold values from 0 to 128, as said below
Outputs:
- density: float32 [8, 64, 64, 128], P('slab', 'dom')
- laplace: float32 [8, 64, 64, 128], P('slab', 'dom')
Inputs may be any that keep to these rules, and one draw needn't show every extreme that they name: `incoming`: positions lie inside the cell that dest assigns to their block, and slots beyond a cell's count hold positions too. dest holds each cell id of the slab exactly once; every block goes to a domain at most 2 indices away along dom, counted cyclically; from one domain exactly 64 blocks go to each of four domains and none to the others. `counts`: the lowest quarter of the z cells are full.
All inputs are finite; a program needn't handle non-finite values.
Results may differ from a plain program's by a relative error of at most 0.0003.
Values sent between devices are 32-bit elements; how exact they have to be, the bound alone decides.
A program may use at most 64 MiB of HBM per device.

v0:
```python
import math

import jax
import jax.numpy as jnp
from jax import lax
from jax.sharding import PartitionSpec as P

radius_eff = 1.0
radius_min = 0.1
ref_density = 268.0825731


def shifted(value, axis, steps):
    count = lax.axis_size(axis)
    pairs = [(source, (source + steps) % count) for source in range(count)]
    return lax.ppermute(value, axis, pairs)


def padded(cells, sides, width):
    for axis, dim in sides:
        count = lax.axis_size(axis)
        ends = count - 1
        head = lax.slice_in_dim(cells, 0, width, axis=dim)
        tail = lax.slice_in_dim(cells, cells.shape[dim] - width, cells.shape[dim], axis=dim)
        cells = jnp.concatenate(
            [
                lax.ppermute(tail, axis, [(i, (i + 1) % count) for i in range(ends)]),
                cells,
                lax.ppermute(head, axis, [((i + 1) % count, i) for i in range(ends)]),
            ],
            axis=dim,
        )
    return cells


def from_behind(block, axis, distance):
    devices = range(lax.axis_size(axis))
    route = [(i - distance, i) for i in devices if i - distance in devices]
    return lax.ppermute(block, axis, route)


def pair_weights(own_cells, own_mask, far_cells, far_mask, diagonal):
    spread = own_cells[:, 0, :, None] - far_cells[:, 0, None, :]
    distance = spread * spread
    for channel in range(1, 3):
        spread = own_cells[:, channel, :, None] - far_cells[:, channel, None, :]
        distance = distance + spread * spread
    radius = jnp.sqrt(jnp.maximum(distance, radius_min * radius_min))
    weight = (
        jnp.maximum(radius_eff / radius - 1.0, 0.0) * own_mask[:, :, None] * far_mask[:, None, :]
    )
    if diagonal:
        weight = weight * (1.0 - jnp.eye(own_mask.shape[1], dtype=weight.dtype))
    return weight


def shell_sums(own_cells, own_mask, far_list, flag_list):
    total_cells = own_cells.shape[0]
    block_width = math.gcd(total_cells, 64)
    groups = total_cells // block_width

    def split_rows(array):
        return array.reshape((groups, block_width) + array.shape[1:])

    far_stacked = tuple(
        ((split_rows(far_part), split_rows(far_flag)) for far_part, far_flag in far_list)
    )

    def one_block(inputs):
        own_part, own_flag, far_pairs = inputs
        outputs = []
        for (far_part, far_flag), (diagonal, with_columns) in zip(far_pairs, flag_list):
            weight = pair_weights(own_part, own_flag, far_part, far_flag, diagonal)
            results = (weight.sum(2), (weight * far_part[:, 3, None, :]).sum(2))
            if with_columns:
                results = results + (weight.sum(1), (weight * own_part[:, 3, :, None]).sum(1))
            outputs.append(results)
        return tuple(outputs)

    mapped = lax.map(one_block, (split_rows(own_cells), split_rows(own_mask), far_stacked))
    return tuple(
        (
            tuple((result.reshape((total_cells,) + result.shape[2:]) for result in results))
            for results in mapped
        )
    )


def local(incoming, dest, counts):
    cells_x, cells_y, cells_z = counts.shape
    slots = incoming.shape[3]
    cell_total = cells_x * cells_y * cells_z
    capacity = cell_total // 4
    domains = lax.axis_size("dom")
    channels = incoming.shape[2] * slots
    blocks = incoming.reshape(cell_total, channels)
    targets = dest.reshape(cell_total)
    target_dom = targets // cell_total
    target_local = (targets % cell_total).astype(jnp.float32)
    my_index = lax.axis_index("dom")
    distance = (target_dom - my_index) % domains
    distance = jnp.where(distance > domains // 2, distance - domains, distance)
    stay_home = distance == 0
    arrived_data = [blocks]
    arrived_index = [jnp.where(stay_home, target_local, -1.0)]
    for offset in (-2, -1, 1, 2):
        chosen = distance == offset
        ranking = jnp.cumsum(chosen.astype(jnp.int32)) - 1
        slot_ids = jnp.where(chosen, ranking, capacity)
        pack_blocks = (
            jnp.zeros((capacity + 1, channels), jnp.float32).at[slot_ids].set(blocks)[:capacity]
        )
        pack_local = (
            jnp.full((capacity + 1,), -1.0, jnp.float32).at[slot_ids].set(target_local)[:capacity]
        )
        got_blocks, got_local = shifted((pack_blocks, pack_local), "dom", offset)
        arrived_data.append(got_blocks)
        arrived_index.append(got_local)
    merged_data = jnp.concatenate(arrived_data, 0)
    merged_index = jnp.concatenate(arrived_index, 0)
    rows_at = jnp.where(merged_index >= 0, merged_index, float(cell_total)).astype(jnp.int32)
    home_cells = (
        jnp.zeros((cell_total + 1, channels), jnp.float32).at[rows_at].set(merged_data)[:cell_total]
    )
    home_cells = home_cells.reshape(cells_x, cells_y, cells_z, channels)
    filled = counts.astype(jnp.float32)
    side_cells, side_count = (
        padded(home_cells, (("dom", 1),), 1),
        padded(filled, (("dom", 1),), 1),
    )
    front_cells, front_count = from_behind((side_cells[0], side_count[0]), "slab", -1)
    padded_grid = jnp.concatenate([side_cells, front_cells[None]], 0)
    grid_count = jnp.concatenate([side_count, front_count[None]], 0)
    start_x = 0
    pair_offsets = [(0, 0, 0), (0, 0, 1)]
    for plane_x, plane_y in ((1, 0), (0, 1), (1, 1), (1, -1)):
        for shift_z in (-1, 0, 1):
            pair_offsets.append((plane_x, plane_y, shift_z))
    padded_grid = jnp.pad(padded_grid, ((0, 0), (0, 0), (1, 1), (0, 0)))
    grid_count = jnp.pad(grid_count, ((0, 0), (0, 0), (1, 1)))
    slot_index = jnp.arange(slots).astype(jnp.float32)
    grid_mask = (slot_index < grid_count[..., None]).astype(jnp.float32)
    grid_cells = padded_grid.reshape(padded_grid.shape[:3] + (4, slots))
    sum_n = jnp.zeros(grid_mask.shape, jnp.float32)
    sum_s = jnp.zeros(grid_mask.shape, jnp.float32)
    own_cells = grid_cells[start_x : start_x + cells_x, 1 : 1 + cells_y, 1 : 1 + cells_z].reshape(
        cell_total, 4, slots
    )
    own_mask = grid_mask[start_x : start_x + cells_x, 1 : 1 + cells_y, 1 : 1 + cells_z].reshape(
        cell_total, slots
    )
    block_shape = (cells_x, cells_y, cells_z, slots)
    far_list = []
    flag_list = []
    for shift_x, shift_y, shift_z in pair_offsets:
        lower_x = start_x + shift_x
        lower_y = 1 + shift_y
        lower_z = 1 + shift_z
        far_cells = grid_cells[
            lower_x : lower_x + cells_x, lower_y : lower_y + cells_y, lower_z : lower_z + cells_z
        ].reshape(cell_total, 4, slots)
        far_mask = grid_mask[
            lower_x : lower_x + cells_x, lower_y : lower_y + cells_y, lower_z : lower_z + cells_z
        ].reshape(cell_total, slots)
        diagonal = shift_x == 0 and shift_y == 0 and (shift_z == 0)
        with_columns = not diagonal
        far_list.append((far_cells, far_mask))
        flag_list.append((diagonal, with_columns))
    all_results = shell_sums(own_cells, own_mask, tuple(far_list), tuple(flag_list))
    for (shift_x, shift_y, shift_z), (diagonal, with_columns), results in zip(
        pair_offsets, flag_list, all_results
    ):
        lower_x = start_x + shift_x
        lower_y = 1 + shift_y
        lower_z = 1 + shift_z
        sum_n = sum_n.at[start_x : start_x + cells_x, 1 : 1 + cells_y, 1 : 1 + cells_z].add(
            results[0].reshape(block_shape)
        )
        sum_s = sum_s.at[start_x : start_x + cells_x, 1 : 1 + cells_y, 1 : 1 + cells_z].add(
            results[1].reshape(block_shape)
        )
        if with_columns:
            sum_n = sum_n.at[
                lower_x : lower_x + cells_x,
                lower_y : lower_y + cells_y,
                lower_z : lower_z + cells_z,
            ].add(results[2].reshape(block_shape))
            sum_s = sum_s.at[
                lower_x : lower_x + cells_x,
                lower_y : lower_y + cells_y,
                lower_z : lower_z + cells_z,
            ].add(results[3].reshape(block_shape))
    back_n, back_s = from_behind((sum_n[cells_x], sum_s[cells_x]), "slab", 1)
    sum_n = sum_n.at[0].add(back_n)
    sum_s = sum_s.at[0].add(back_s)
    lower_n, lower_s = from_behind((sum_n[:cells_x, 0], sum_s[:cells_x, 0]), "dom", -1)
    sum_n = sum_n.at[:cells_x, cells_y].add(lower_n)
    sum_s = sum_s.at[:cells_x, cells_y].add(lower_s)
    upper_n, upper_s = from_behind(
        (sum_n[:cells_x, cells_y + 1], sum_s[:cells_x, cells_y + 1]), "dom", 1
    )
    sum_n = sum_n.at[:cells_x, 1].add(upper_n)
    sum_s = sum_s.at[:cells_x, 1].add(upper_s)
    totals_n = sum_n[start_x : start_x + cells_x, 1 : 1 + cells_y, 1 : 1 + cells_z]
    totals_s = sum_s[start_x : start_x + cells_x, 1 : 1 + cells_y, 1 : 1 + cells_z]
    potential = home_cells[..., 3 * slots : 4 * slots]
    density = totals_n / ref_density
    laplace = (totals_s - potential * totals_n) / ref_density
    return (density, laplace)


def solution(mesh):
    in_specs = (P("slab", "dom", None, None), P("slab", "dom"), P("slab", "dom", None))
    out_specs = (P("slab", "dom", None, None), P("slab", "dom", None, None))
    return jax.shard_map(local, mesh=mesh, in_specs=in_specs, out_specs=out_specs, check_vma=False)
```

profile of v0, /device:TPU:1, one launch (start us, length us, event | category | flops | bytes accessed | tf_op | source)
XLA Modules:
  0.0 654.8 jit_solution(2204329644942026008)
XLA Ops:
  12.5 9.1 %collective-permute-start = (f32[64]{0:T(128)S(1)}, f32[64]{0:T(128)S(1)}, u32[]{:S(2)}, u32[]{:S(2)}) collective-permute-start(f32[64]{0:T(128)S(1)} %bitcast.735), channel_id=1, source_target_pairs={{0,30},{1,31},{2,0},{3,1},{4,2},{5,3},{6,4},{7,5},{8,6},{9,7},{10,... | collective-permute-start | bytes 776 | tf_op jit(solution)/shard_map/ppermute | solution.py:16
  25.1 4.8 collective-permute-start.4
  62.7 10.6 %collective-permute-done.10 = f32[4,64,512]{2,1,0:T(8,128)S(1)} collective-permute-done((f32[4,64,512]{2,1,0:T(8,128)S(1)}, f32[4,64,512]{2,1,0:T(8,128)S(1)}, u32[]{:S(2)}, u32[]{:S(2)}) %collective-permute-start.10) | collective-permute-done | bytes 524320 | tf_op jit(solution)/shard_map/ppermute | solution.py:39
  86.0 517.9 %while.180 = (s32[]{:T(128)}, f32[4,64,128]{2,1,0:T(8,128)}, f32[4,64,128]{2,1,0:T(8,128)}, f32[4,64,128]{2,1,0:T(8,128)}, f32[4,64,128]{2,1,0:T(8,128)}, /*inde...) while((s32[]{:T(128)}, f32[4,64,128]{2,1,0:T(8,128)}, ...), condition=%wide.region_72.73_spmd, body=%wide.region_17.72_spmd.sunk | while | flops 276430848 | bytes 17002220 | solution.py:80
  90.3 12.4 %multiply_reduce_fusion.37 = (f32[64,128]{1,0:T(8,128)S(1)}, f32[64,128]{1,0:T(8,128)S(1)}, f32[64,128]{1,0:T(8,128)S(1)}, f32[64,128]{1,0:T(8,128)S(1)}, f32[64...) fusion(f32[64,128]{1,0:T(8,128)S(1)} %get-tuple-element.3216, ...), kind=kLoop, calls=%fused_computation.15.clone.1 | loop fusion | flops 39780352 | bytes 753664 | tf_op jit(solution)/shard_map/while/body/eval_jaxpr/reduce_sum | solution.py:76
  105.2 12.4 %multiply_reduce_fusion.38 = (f32[64,128]{1,0:T(8,128)S(1)}, f32[64,128]{1,0:T(8,128)S(1)}, f32[64,128]{1,0:T(8,128)S(1)}, f32[64,128]{1,0:T(8,128)S(1)}, f32[64...) fusion(f32[64,128]{1,0:T(8,128)S(1)} %get-tuple-element.3216, ...), kind=kLoop, calls=%fused_computation.18.clone.1 | loop fusion | flops 39780352 | bytes 753664 | tf_op jit(solution)/shard_map/while/body/eval_jaxpr/reduce_sum | solution.py:76
  123.6 12.4 %multiply_reduce_fusion.39 = (f32[64,128]{1,0:T(8,128)S(1)}, f32[64,128]{1,0:T(8,128)S(1)}, f32[64,128]{1,0:T(8,128)S(1)}, f32[64,128]{1,0:T(8,128)S(1)}, f32[64...) fusion(f32[64,128]{1,0:T(8,128)S(1)} %get-tuple-element.3216, ...), kind=kLoop, calls=%fused_computation.21.clone.1 | loop fusion | flops 39780352 | bytes 753664 | tf_op jit(solution)/shard_map/while/body/eval_jaxpr/reduce_sum | solution.py:76
  138.5 12.4 %multiply_reduce_fusion.40 = (f32[64,128]{1,0:T(8,128)S(1)}, f32[64,128]{1,0:T(8,128)S(1)}, f32[64,128]{1,0:T(8,128)S(1)}, f32[64,128]{1,0:T(8,128)S(1)}, f32[64...) fusion(f32[64,128]{1,0:T(8,128)S(1)} %get-tuple-element.3216, ...), kind=kLoop, calls=%fused_computation.24.clone.1 | loop fusion | flops 39780352 | bytes 753664 | tf_op jit(solution)/shard_map/while/body/eval_jaxpr/reduce_sum | solution.py:76
  164.8 12.4 %multiply_reduce_fusion.36 = (f32[64,128]{1,0:T(8,128)S(1)}, f32[64,128]{1,0:T(8,128)S(1)}, f32[64,128]{1,0:T(8,128)S(1)}, f32[64,128]{1,0:T(8,128)S(1)}, f32[64...) fusion(f32[64,128]{1,0:T(8,128)S(1)} %get-tuple-element.3216, ...), kind=kLoop, calls=%fused_computation.12.clone.1 | loop fusion | flops 39780352 | bytes 753664 | tf_op jit(solution)/shard_map/while/body/eval_jaxpr/reduce_sum | solution.py:76
  182.1 9.7 %multiply_reduce_fusion.35 = (f32[64,128]{1,0:T(8,128)S(1)}, f32[64,128]{1,0:T(8,128)S(1)}, f32[64,128]{1,0:T(8,128)S(1)}, f32[64,128]{1,0:T(8,128)S(1)}) fusion(f32[64,128]{1,0:T(8,128)S(1)} %get-tuple-element.3216, f32[64,128]{1,0:T(8,128)S(1)} %get-tuple-element.3235, f32[64,128]{1,0:T(8,128)S(1)} %get-tuple-element.3218, ...), kind=kLoop, calls=%fused_computation.45.clone.1 | loop fusion | flops 19890176 | bytes 458752 | tf_op jit(solution)/shard_map/while/body/eval_jaxpr/reduce_sum | solution.py:76
  194.2 15.0 %multiply_reduce_fusion.34 = (f32[64,128]{1,0:T(8,128)S(1)}, f32[64,128]{1,0:T(8,128)S(1)}, f32[64,128]{1,0:T(8,128)S(1)}, f32[64,128]{1,0:T(8,128)S(1)}, f32[64...) fusion(f32[64,128]{1,0:T(8,128)S(1)} %get-tuple-element.3216, ...), kind=kLoop, calls=%fused_computation.9.clone.1 | loop fusion | flops 57589760 | bytes 884736 | tf_op jit(solution)/shard_map/while/body/eval_jaxpr/reduce_sum | solution.py:76
  219.7 12.4 %multiply_reduce_fusion.37 = (f32[64,128]{1,0:T(8,128)S(1)}, f32[64,128]{1,0:T(8,128)S(1)}, f32[64,128]{1,0:T(8,128)S(1)}, f32[64,128]{1,0:T(8,128)S(1)}, f32[64...) fusion(f32[64,128]{1,0:T(8,128)S(1)} %get-tuple-element.3216, ...), kind=kLoop, calls=%fused_computation.15.clone.1 | loop fusion | flops 39780352 | bytes 753664 | tf_op jit(solution)/shard_map/while/body/eval_jaxpr/reduce_sum | solution.py:76
  234.5 12.4 %multiply_reduce_fusion.38 = (f32[64,128]{1,0:T(8,128)S(1)}, f32[64,128]{1,0:T(8,128)S(1)}, f32[64,128]{1,0:T(8,128)S(1)}, f32[64,128]{1,0:T(8,128)S(1)}, f32[64...) fusion(f32[64,128]{1,0:T(8,128)S(1)} %get-tuple-element.3216, ...), kind=kLoop, calls=%fused_computation.18.clone.1 | loop fusion | flops 39780352 | bytes 753664 | tf_op jit(solution)/shard_map/while/body/eval_jaxpr/reduce_sum | solution.py:76
  253.0 12.4 %multiply_reduce_fusion.39 = (f32[64,128]{1,0:T(8,128)S(1)}, f32[64,128]{1,0:T(8,128)S(1)}, f32[64,128]{1,0:T(8,128)S(1)}, f32[64,128]{1,0:T(8,128)S(1)}, f32[64...) fusion(f32[64,128]{1,0:T(8,128)S(1)} %get-tuple-element.3216, ...), kind=kLoop, calls=%fused_computation.21.clone.1 | loop fusion | flops 39780352 | bytes 753664 | tf_op jit(solution)/shard_map/while/body/eval_jaxpr/reduce_sum | solution.py:76
  267.9 12.4 %multiply_reduce_fusion.40 = (f32[64,128]{1,0:T(8,128)S(1)}, f32[64,128]{1,0:T(8,128)S(1)}, f32[64,128]{1,0:T(8,128)S(1)}, f32[64,128]{1,0:T(8,128)S(1)}, f32[64...) fusion(f32[64,128]{1,0:T(8,128)S(1)} %get-tuple-element.3216, ...), kind=kLoop, calls=%fused_computation.24.clone.1 | loop fusion | flops 39780352 | bytes 753664 | tf_op jit(solution)/shard_map/while/body/eval_jaxpr/reduce_sum | solution.py:76
  294.3 12.4 %multiply_reduce_fusion.36 = (f32[64,128]{1,0:T(8,128)S(1)}, f32[64,128]{1,0:T(8,128)S(1)}, f32[64,128]{1,0:T(8,128)S(1)}, f32[64,128]{1,0:T(8,128)S(1)}, f32[64...) fusion(f32[64,128]{1,0:T(8,128)S(1)} %get-tuple-element.3216, ...), kind=kLoop, calls=%fused_computation.12.clone.1 | loop fusion | flops 39780352 | bytes 753664 | tf_op jit(solution)/shard_map/while/body/eval_jaxpr/reduce_sum | solution.py:76
  311.6 9.7 %multiply_reduce_fusion.35 = (f32[64,128]{1,0:T(8,128)S(1)}, f32[64,128]{1,0:T(8,128)S(1)}, f32[64,128]{1,0:T(8,128)S(1)}, f32[64,128]{1,0:T(8,128)S(1)}) fusion(f32[64,128]{1,0:T(8,128)S(1)} %get-tuple-element.3216, f32[64,128]{1,0:T(8,128)S(1)} %get-tuple-element.3235, f32[64,128]{1,0:T(8,128)S(1)} %get-tuple-element.3218, ...), kind=kLoop, calls=%fused_computation.45.clone.1 | loop fusion | flops 19890176 | bytes 458752 | tf_op jit(solution)/shard_map/while/body/eval_jaxpr/reduce_sum | solution.py:76
  323.8 15.0 %multiply_reduce_fusion.34 = (f32[64,128]{1,0:T(8,128)S(1)}, f32[64,128]{1,0:T(8,128)S(1)}, f32[64,128]{1,0:T(8,128)S(1)}, f32[64,128]{1,0:T(8,128)S(1)}, f32[64...) fusion(f32[64,128]{1,0:T(8,128)S(1)} %get-tuple-element.3216, ...), kind=kLoop, calls=%fused_computation.9.clone.1 | loop fusion | flops 57589760 | bytes 884736 | tf_op jit(solution)/shard_map/while/body/eval_jaxpr/reduce_sum | solution.py:76
  349.2 12.4 %multiply_reduce_fusion.37 = (f32[64,128]{1,0:T(8,128)S(1)}, f32[64,128]{1,0:T(8,128)S(1)}, f32[64,128]{1,0:T(8,128)S(1)}, f32[64,128]{1,0:T(8,128)S(1)}, f32[64...) fusion(f32[64,128]{1,0:T(8,128)S(1)} %get-tuple-element.3216, ...), kind=kLoop, calls=%fused_computation.15.clone.1 | loop fusion | flops 39780352 | bytes 753664 | tf_op jit(solution)/shard_map/while/body/eval_jaxpr/reduce_sum | solution.py:76
  364.1 12.4 %multiply_reduce_fusion.38 = (f32[64,128]{1,0:T(8,128)S(1)}, f32[64,128]{1,0:T(8,128)S(1)}, f32[64,128]{1,0:T(8,128)S(1)}, f32[64,128]{1,0:T(8,128)S(1)}, f32[64...) fusion(f32[64,128]{1,0:T(8,128)S(1)} %get-tuple-element.3216, ...), kind=kLoop, calls=%fused_computation.18.clone.1 | loop fusion | flops 39780352 | bytes 753664 | tf_op jit(solution)/shard_map/while/body/eval_jaxpr/reduce_sum | solution.py:76
  382.5 12.4 %multiply_reduce_fusion.39 = (f32[64,128]{1,0:T(8,128)S(1)}, f32[64,128]{1,0:T(8,128)S(1)}, f32[64,128]{1,0:T(8,128)S(1)}, f32[64,128]{1,0:T(8,128)S(1)}, f32[64...) fusion(f32[64,128]{1,0:T(8,128)S(1)} %get-tuple-element.3216, ...), kind=kLoop, calls=%fused_computation.21.clone.1 | loop fusion | flops 39780352 | bytes 753664 | tf_op jit(solution)/shard_map/while/body/eval_jaxpr/reduce_sum | solution.py:76
  397.4 12.4 %multiply_reduce_fusion.40 = (f32[64,128]{1,0:T(8,128)S(1)}, f32[64,128]{1,0:T(8,128)S(1)}, f32[64,128]{1,0:T(8,128)S(1)}, f32[64,128]{1,0:T(8,128)S(1)}, f32[64...) fusion(f32[64,128]{1,0:T(8,128)S(1)} %get-tuple-element.3216, ...), kind=kLoop, calls=%fused_computation.24.clone.1 | loop fusion | flops 39780352 | bytes 753664 | tf_op jit(solution)/shard_map/while/body/eval_jaxpr/reduce_sum | solution.py:76
  423.8 12.4 %multiply_reduce_fusion.36 = (f32[64,128]{1,0:T(8,128)S(1)}, f32[64,128]{1,0:T(8,128)S(1)}, f32[64,128]{1,0:T(8,128)S(1)}, f32[64,128]{1,0:T(8,128)S(1)}, f32[64...) fusion(f32[64,128]{1,0:T(8,128)S(1)} %get-tuple-element.3216, ...), kind=kLoop, calls=%fused_computation.12.clone.1 | loop fusion | flops 39780352 | bytes 753664 | tf_op jit(solution)/shard_map/while/body/eval_jaxpr/reduce_sum | solution.py:76
  441.0 9.7 %multiply_reduce_fusion.35 = (f32[64,128]{1,0:T(8,128)S(1)}, f32[64,128]{1,0:T(8,128)S(1)}, f32[64,128]{1,0:T(8,128)S(1)}, f32[64,128]{1,0:T(8,128)S(1)}) fusion(f32[64,128]{1,0:T(8,128)S(1)} %get-tuple-element.3216, f32[64,128]{1,0:T(8,128)S(1)} %get-tuple-element.3235, f32[64,128]{1,0:T(8,128)S(1)} %get-tuple-element.3218, ...), kind=kLoop, calls=%fused_computation.45.clone.1 | loop fusion | flops 19890176 | bytes 458752 | tf_op jit(solution)/shard_map/while/body/eval_jaxpr/reduce_sum | solution.py:76
  453.2 15.0 %multiply_reduce_fusion.34 = (f32[64,128]{1,0:T(8,128)S(1)}, f32[64,128]{1,0:T(8,128)S(1)}, f32[64,128]{1,0:T(8,128)S(1)}, f32[64,128]{1,0:T(8,128)S(1)}, f32[64...) fusion(f32[64,128]{1,0:T(8,128)S(1)} %get-tuple-element.3216, ...), kind=kLoop, calls=%fused_computation.9.clone.1 | loop fusion | flops 57589760 | bytes 884736 | tf_op jit(solution)/shard_map/while/body/eval_jaxpr/reduce_sum | solution.py:76
  478.6 12.4 %multiply_reduce_fusion.37 = (f32[64,128]{1,0:T(8,128)S(1)}, f32[64,128]{1,0:T(8,128)S(1)}, f32[64,128]{1,0:T(8,128)S(1)}, f32[64,128]{1,0:T(8,128)S(1)}, f32[64...) fusion(f32[64,128]{1,0:T(8,128)S(1)} %get-tuple-element.3216, ...), kind=kLoop, calls=%fused_computation.15.clone.1 | loop fusion | flops 39780352 | bytes 753664 | tf_op jit(solution)/shard_map/while/body/eval_jaxpr/reduce_sum | solution.py:76
  493.5 12.4 %multiply_reduce_fusion.38 = (f32[64,128]{1,0:T(8,128)S(1)}, f32[64,128]{1,0:T(8,128)S(1)}, f32[64,128]{1,0:T(8,128)S(1)}, f32[64,128]{1,0:T(8,128)S(1)}, f32[64...) fusion(f32[64,128]{1,0:T(8,128)S(1)} %get-tuple-element.3216, ...), kind=kLoop, calls=%fused_computation.18.clone.1 | loop fusion | flops 39780352 | bytes 753664 | tf_op jit(solution)/shard_map/while/body/eval_jaxpr/reduce_sum | solution.py:76
  512.0 12.4 %multiply_reduce_fusion.39 = (f32[64,128]{1,0:T(8,128)S(1)}, f32[64,128]{1,0:T(8,128)S(1)}, f32[64,128]{1,0:T(8,128)S(1)}, f32[64,128]{1,0:T(8,128)S(1)}, f32[64...) fusion(f32[64,128]{1,0:T(8,128)S(1)} %get-tuple-element.3216, ...), kind=kLoop, calls=%fused_computation.21.clone.1 | loop fusion | flops 39780352 | bytes 753664 | tf_op jit(solution)/shard_map/while/body/eval_jaxpr/reduce_sum | solution.py:76
  526.8 12.4 %multiply_reduce_fusion.40 = (f32[64,128]{1,0:T(8,128)S(1)}, f32[64,128]{1,0:T(8,128)S(1)}, f32[64,128]{1,0:T(8,128)S(1)}, f32[64,128]{1,0:T(8,128)S(1)}, f32[64...) fusion(f32[64,128]{1,0:T(8,128)S(1)} %get-tuple-element.3216, ...), kind=kLoop, calls=%fused_computation.24.clone.1 | loop fusion | flops 39780352 | bytes 753664 | tf_op jit(solution)/shard_map/while/body/eval_jaxpr/reduce_sum | solution.py:76
  553.2 12.4 %multiply_reduce_fusion.36 = (f32[64,128]{1,0:T(8,128)S(1)}, f32[64,128]{1,0:T(8,128)S(1)}, f32[64,128]{1,0:T(8,128)S(1)}, f32[64,128]{1,0:T(8,128)S(1)}, f32[64...) fusion(f32[64,128]{1,0:T(8,128)S(1)} %get-tuple-element.3216, ...), kind=kLoop, calls=%fused_computation.12.clone.1 | loop fusion | flops 39780352 | bytes 753664 | tf_op jit(solution)/shard_map/while/body/eval_jaxpr/reduce_sum | solution.py:76
  570.5 9.7 %multiply_reduce_fusion.35 = (f32[64,128]{1,0:T(8,128)S(1)}, f32[64,128]{1,0:T(8,128)S(1)}, f32[64,128]{1,0:T(8,128)S(1)}, f32[64,128]{1,0:T(8,128)S(1)}) fusion(f32[64,128]{1,0:T(8,128)S(1)} %get-tuple-element.3216, f32[64,128]{1,0:T(8,128)S(1)} %get-tuple-element.3235, f32[64,128]{1,0:T(8,128)S(1)} %get-tuple-element.3218, ...), kind=kLoop, calls=%fused_computation.45.clone.1 | loop fusion | flops 19890176 | bytes 458752 | tf_op jit(solution)/shard_map/while/body/eval_jaxpr/reduce_sum | solution.py:76
  582.7 15.0 %multiply_reduce_fusion.34 = (f32[64,128]{1,0:T(8,128)S(1)}, f32[64,128]{1,0:T(8,128)S(1)}, f32[64,128]{1,0:T(8,128)S(1)}, f32[64,128]{1,0:T(8,128)S(1)}, f32[64...) fusion(f32[64,128]{1,0:T(8,128)S(1)} %get-tuple-element.3216, ...), kind=kLoop, calls=%fused_computation.9.clone.1 | loop fusion | flops 57589760 | bytes 884736 | tf_op jit(solution)/shard_map/while/body/eval_jaxpr/reduce_sum | solution.py:76
  (722 shorter events, 279.0 us)
Async XLA Ops:
  0.6 30.4 %copy-start = (f32[1,256,4,128]{3,2,1,0:T(4,128)S(1)}, f32[1,256,4,128]{3,2,1,0:T(4,128)}, u32[]{:S(2)}) copy-start(f32[1,256,4,128]{3,2,1,0:T(4,128)} %param.125) | copy-start | bytes 1572868
  0.6 31.9 %copy-start.52 = (s32[2,2,64]{2,1,0:T(2,128)S(1)}, s32[2,2,64]{2,1,0:T(2,128)}, u32[]{:S(2)}) copy-start(s32[2,2,64]{2,1,0:T(2,128)} %param.127) | copy-start | bytes 3076
  6.5 31.0 %collective-permute-start.1 = (f32[64]{0:T(128)S(1)}, f32[64]{0:T(128)S(1)}, u32[]{:S(2)}, u32[]{:S(2)}) collective-permute-start(f32[64]{0:T(128)S(1)} %bitcast.737), channel_id=1, source_target_pairs={{0,31},{1,0},{2,1},{3,2},{4,3},{5,4},{6,5},{7,6},{8,7},{9,8},{10,9... | collective-permute-start | bytes 776 | tf_op jit(solution)/shard_map/ppermute | solution.py:16
  9.4 28.2 %collective-permute-start.2 = (f32[64]{0:T(128)S(1)}, f32[64]{0:T(128)S(1)}, u32[]{:S(2)}, u32[]{:S(2)}) collective-permute-start(f32[64]{0:T(128)S(1)} %bitcast.736), channel_id=1, source_target_pairs={{0,1},{1,2},{2,3},{3,4},{4,5},{5,6},{6,7},{7,8},{8,9},{9,10},{10,1... | collective-permute-start | bytes 776 | tf_op jit(solution)/shard_map/ppermute | solution.py:16
  12.5 26.8 %collective-permute-start = (f32[64]{0:T(128)S(1)}, f32[64]{0:T(128)S(1)}, u32[]{:S(2)}, u32[]{:S(2)}) collective-permute-start(f32[64]{0:T(128)S(1)} %bitcast.735), channel_id=1, source_target_pairs={{0,30},{1,31},{2,0},{3,1},{4,2},{5,3},{6,4},{7,5},{8,6},{9,7},{10,... | collective-permute-start | bytes 776 | tf_op jit(solution)/shard_map/ppermute | solution.py:16
  23.0 16.3 %collective-permute-start.3 = (f32[64]{0:T(128)S(1)}, f32[64]{0:T(128)S(1)}, u32[]{:S(2)}, u32[]{:S(2)}) collective-permute-start(f32[64]{0:T(128)S(1)} %bitcast.734), channel_id=1, source_target_pairs={{0,2},{1,3},{2,4},{3,5},{4,6},{5,7},{6,8},{7,9},{8,10},{9,11},{10,... | collective-permute-start | bytes 776 | tf_op jit(solution)/shard_map/ppermute | solution.py:16
  25.1 16.3 %collective-permute-start.4 = (f32[64,512]{1,0:T(8,128)S(1)}, f32[64,512]{1,0:T(8,128)S(1)}, u32[]{:S(2)}, u32[]{:S(2)}) collective-permute-start(f32[64,512]{1,0:T(8,128)S(1)} %slice.3001), channel_id=1, source_target_pairs={{0,30},{1,31},{2,0},{3,1},{4,2},{5,3},{6,4},{7,5},{8,6},{9,7},{10,... | collective-permute-start | bytes 393224 | tf_op jit(solution)/shard_map/ppermute | solution.py:16
  37.5 6.5 collective-permute-start.5
  37.6 6.4 collective-permute-start.6
  39.3 8.5 %collective-permute-start.7 = (f32[64,512]{1,0:T(8,128)S(1)}, f32[64,512]{1,0:T(8,128)S(1)}, u32[]{:S(2)}, u32[]{:S(2)}) collective-permute-start(f32[64,512]{1,0:T(8,128)S(1)} %slice.3004), channel_id=1, source_target_pairs={{0,2},{1,3},{2,4},{3,5},{4,6},{5,7},{6,8},{7,9},{8,10},{9,11},{10,... | collective-permute-start | bytes 393224 | tf_op jit(solution)/shard_map/ppermute | solution.py:16
  39.3 16.5 %collective-permute-start.11 = (f32[2,1,64]{2,1,0:T(1,128)S(1)}, f32[2,1,64]{2,1,0:T(1,128)S(1)}, u32[]{:S(2)}, u32[]{:S(2)}) collective-permute-start(f32[2,1,64]{2,1,0:T(1,128)S(1)} %get-tuple-element.2559), channel_id=1, source_target_pairs={{0,1},{1,2},{2,3},{3,4},{4,5},{5,6},{6,7},{7,8},{8,9},{9,10},{10,1... | collective-permute-start | bytes 1544 | tf_op jit(solution)/shard_map/ppermute | solution.py:27
  41.5 14.4 %collective-permute-start.12 = (f32[2,1,64]{2,1,0:T(1,128)S(1)}, f32[2,1,64]{2,1,0:T(1,128)S(1)}, u32[]{:S(2)}, u32[]{:S(2)}) collective-permute-start(f32[2,1,64]{2,1,0:T(1,128)S(1)} %get-tuple-element.2560), channel_id=1, source_target_pairs={{1,0},{2,1},{3,2},{4,3},{5,4},{6,5},{7,6},{8,7},{9,8},{10,9},{11,1... | collective-permute-start | bytes 1544 | tf_op jit(solution)/shard_map/ppermute | solution.py:29
  44.0 11.1 %copy-start.53 = (s32[4]{0:T(128)S(1)}, s32[4]{0:T(128)}, u32[]{:S(2)}) copy-start(s32[4]{0:T(128)} %constant.1668.clone.1) | copy-start | bytes 52
  50.3 6.9 %collective-permute-start.8 = (f32[2,1,64,512]{3,2,1,0:T(8,128)S(1)}, f32[2,1,64,512]{3,2,1,0:T(8,128)S(1)}, u32[]{:S(2)}, u32[]{:S(2)}) collective-permute-start(f32[2,1,64,512]{3,2,1,0:T(8,128)S(1)} %get-tuple-element.2541), channel_id=1, source_target_pairs={{0,1},{1,2},{2,3},{3,4},{4,5},{5,6},{6,7},{7,8},{8,9},{9,10},{10,1... | collective-permute-start | bytes 786440 | tf_op jit(solution)/shard_map/ppermute | solution.py:27
  52.2 7.7 %collective-permute-start.9 = (f32[2,1,64,512]{3,2,1,0:T(8,128)S(1)}, f32[2,1,64,512]{3,2,1,0:T(8,128)S(1)}, u32[]{:S(2)}, u32[]{:S(2)}) collective-permute-start(f32[2,1,64,512]{3,2,1,0:T(8,128)S(1)} %get-tuple-element.2542), channel_id=1, source_target_pairs={{1,0},{2,1},{3,2},{4,3},{5,4},{6,5},{7,6},{8,7},{9,8},{10,9},{11,1... | collective-permute-start | bytes 786440 | tf_op jit(solution)/shard_map/ppermute | solution.py:29
  55.9 5.3 collective-permute-start.13
  60.0 13.3 %collective-permute-start.10 = (f32[4,64,512]{2,1,0:T(8,128)S(1)}, f32[4,64,512]{2,1,0:T(8,128)S(1)}, u32[]{:S(2)}, u32[]{:S(2)}) collective-permute-start(f32[4,64,512]{2,1,0:T(8,128)S(1)} %fusion.36), channel_id=1, source_target_pairs={{32,0},{64,32},{96,64},{33,1},{65,33},{97,65},{34,2},{66,34},{98,6... | collective-permute-start | bytes 1572872 | tf_op jit(solution)/shard_map/ppermute | solution.py:39
  603.8 7.2 %copy-start.48 = (f32[4,64,128]{2,1,0:T(8,128)S(1)}, f32[4,64,128]{2,1,0:T(8,128)}, u32[]{:S(2)}) copy-start(f32[4,64,128]{2,1,0:T(8,128)} %get-tuple-element.2140) | copy-start | bytes 393220
  603.8 7.5 %copy-start.50 = (f32[4,64,128]{2,1,0:T(8,128)S(1)}, f32[4,64,128]{2,1,0:T(8,128)}, u32[]{:S(2)}) copy-start(f32[4,64,128]{2,1,0:T(8,128)} %get-tuple-element.2141) | copy-start | bytes 393220
  603.8 7.6 %copy-start.3 = (f32[4,64,128]{2,1,0:T(8,128)S(1)}, f32[4,64,128]{2,1,0:T(8,128)}, u32[]{:S(2)}) copy-start(f32[4,64,128]{2,1,0:T(8,128)} %get-tuple-element.2142) | copy-start | bytes 393220
  603.8 7.9 %copy-start.5 = (f32[4,64,128]{2,1,0:T(8,128)S(1)}, f32[4,64,128]{2,1,0:T(8,128)}, u32[]{:S(2)}) copy-start(f32[4,64,128]{2,1,0:T(8,128)} %get-tuple-element.2143) | copy-start | bytes 393220
  604.8 7.3 %copy-start.7 = (f32[4,64,128]{2,1,0:T(8,128)S(1)}, f32[4,64,128]{2,1,0:T(8,128)}, u32[]{:S(2)}) copy-start(f32[4,64,128]{2,1,0:T(8,128)} %get-tuple-element.2144) | copy-start | bytes 393220
  606.2 6.3 copy-start.9
  618.0 8.5 %copy-start.49 = (f32[4,64,128]{2,1,0:T(8,128)S(1)}, f32[4,64,128]{2,1,0:T(8,128)}, u32[]{:S(2)}) copy-start(f32[4,64,128]{2,1,0:T(8,128)} %get-tuple-element.2167) | copy-start | bytes 393220
  618.3 8.6 %copy-start.2 = (f32[4,64,128]{2,1,0:T(8,128)S(1)}, f32[4,64,128]{2,1,0:T(8,128)}, u32[]{:S(2)}) copy-start(f32[4,64,128]{2,1,0:T(8,128)} %get-tuple-element.2168) | copy-start | bytes 393220
  618.3 8.6 %copy-start.4 = (f32[4,64,128]{2,1,0:T(8,128)S(1)}, f32[4,64,128]{2,1,0:T(8,128)}, u32[]{:S(2)}) copy-start(f32[4,64,128]{2,1,0:T(8,128)} %get-tuple-element.2169) | copy-start | bytes 393220
  618.4 18.4 %collective-permute-start.14 = (f32[4,66,128]{2,1,0:T(8,128)S(1)}, f32[4,66,128]{2,1,0:T(8,128)S(1)}, u32[]{:S(2)}, u32[]{:S(2)}) collective-permute-start(f32[4,66,128]{2,1,0:T(8,128)S(1)} %slice_bitcast_fusion.58), channel_id=1, source_target_pairs={{0,32},{32,64},{64,96},{1,33},{33,65},{65,97},{2,34},{34,66},{66,9... | collective-permute-start | bytes 405512 | tf_op jit(solution)/shard_map/ppermute | solution.py:39
  633.6 6.4 collective-permute-start.17
  636.8 5.7 collective-permute-start.15
  640.1 7.4 %collective-permute-start.18 = (f32[2,66,128]{2,1,0:T(8,128)S(1)}, f32[2,66,128]{2,1,0:T(8,128)S(1)}, u32[]{:S(2)}, u32[]{:S(2)}) collective-permute-start(f32[2,66,128]{2,1,0:T(8,128)S(1)} %slice_bitcast_fusion.61), channel_id=1, source_target_pairs={{1,0},{2,1},{3,2},{4,3},{5,4},{6,5},{7,6},{8,7},{9,8},{10,9},{11,1... | collective-permute-start | bytes 202760 | tf_op jit(solution)/shard_map/ppermute | solution.py:39
  644.3 7.0 %collective-permute-start.16 = (f32[2,66,128]{2,1,0:T(8,128)S(1)}, f32[2,66,128]{2,1,0:T(8,128)S(1)}, u32[]{:S(2)}, u32[]{:S(2)}) collective-permute-start(f32[2,66,128]{2,1,0:T(8,128)S(1)} %slice_bitcast_fusion.62), channel_id=1, source_target_pairs={{0,1},{1,2},{2,3},{3,4},{4,5},{5,6},{6,7},{7,8},{8,9},{9,10},{10,1... | collective-permute-start | bytes 202760 | tf_op jit(solution)/shard_map/ppermute | solution.py:39
  649.4 3.3 collective-permute-start.19
  (42 other events, 95.3 us)
where the time goes:
time: 658 us; the launch traced here: 655 us
  other arithmetic  367 us (56%)
  local copies, waits for them, and re-layouts  218 us (33%)
  starting transfers between devices  46.4 us (7%)
  waiting for transfers between devices  18.9 us (3%)
    reduce_sum x28, other arithmetic, one_block(): (weight * own_part[:, 3, :, None]).sum(1)  347 us
    dynamic_update_slice x216, local copies, waits for them, and re-layouts, shell_sums(): lax.map(one_block, (split_rows(own_cells), split_rows(own_mask), far_stac...  131 us
    squeeze x28, local copies, waits for them, and re-layouts, shell_sums(): lax.map(one_block, (split_rows(own_cells), split_rows(own_mask), far_stac...  19.7 us
    ppermute x8, starting transfers between devices, shifted(): return lax.ppermute(value, axis, pairs)  19 us
    mul x28, local copies, waits for them, and re-layouts, pair_weights(): jnp.maximum(radius_eff / radius - 1.0, 0.0) * own_mask[:, :, None]  18.8 us
    ppermute x8, starting transfers between devices, from_behind(): return lax.ppermute(block, axis, route)  18.5 us
  transfers between devices with their start and end apart: 20, of which 6 were waited for; matrix products, arithmetic and copies ran while one was open for 5% of the time, Pallas kernels for 0%

commit v1 on v0

v1 whole, which is shorter than its diff:
```python
import functools
import jax, jax.numpy as jnp
from jax import lax
from jax.experimental import pallas as pl
from jax.experimental.pallas import tpu as pltpu
from jax.sharding import PartitionSpec as P

f32, bf16 = jnp.float32, jnp.bfloat16
SENT = 100.0
ZP = 66
ref_density = 268.0825731

OFFS = [(0, 0, 0), (0, 0, 1)] + [(dx, dy, dz) for dx, dy in ((0, 1), (1, -1), (1, 0), (1, 1)) for dz in (-1, 0, 1)]
NT = len(OFFS)


def split3(v):
    h = v.astype(bf16).astype(f32)
    r = v - h
    m = r.astype(bf16).astype(f32)
    return h, m, r - m


def left(h, m, l):
    return [h, h, m, m, h, l]


def right(h, m, l):
    return [h, m, h, m, l, h]


def build_cols(p_ref, row0, col, x0, y0, own_cell, b_ref, f_ref, a_ref, stage, stage_a):
    @pl.loop(0, 8)
    def _(k):
        z0 = k * 8
        rows = pl.ds(pl.multiple_of(row0 + z0, 8), 8)
        x = p_ref[rows, 0:128] - x0
        y = p_ref[rows, 128:256] - y0
        zc = (lax.broadcasted_iota(jnp.int32, (8, 128), 0) + z0).astype(f32) + 0.5
        z = p_ref[rows, 256:384] - zc
        f = p_ref[rows, 384:512]
        f_ref[pl.ds(col * ZP + 1 + z0, 8), :] = f
        one = jnp.ones_like(x)
        sx, sy, sz = split3(x), split3(y), split3(z)
        xy = x * x + y * y
        terms = right(*sx) + right(*sy) + list(split3(xy + z * z)) + [None] + right(*sz) + [one] * 3
        for r, v in enumerate(terms):
            if v is not None:
                stage[pl.ds(r, 8, stride=32), :] = v
        b_ref[pl.ds(pl.multiple_of((col * ZP + 1 + z0) * 32, 32), 256), :] = stage[...].astype(bf16)
        if own_cell is None:
            return
        terms = [-2.0 * v for v in left(*sx)] + [-2.0 * v for v in left(*sy)] + [one] * 3 + [None]
        for s in (-1.0, 0.0, 1.0):
            zs = z - s
            terms += [-2.0 * v for v in left(*split3(zs))] + list(split3(xy + zs * zs))
            terms += (list(split3(f)) if s < 0 else [None] * 3) + [None] * 4
        for r, v in enumerate(terms):
            if v is not None:
                stage_a[pl.ds(r, 8, stride=64), :] = v
        for j in range(8):
            t = stage_a[j * 64:j * 64 + 64, :].T
            a_ref[pl.ds(pl.multiple_of((own_cell + z0 + j) * 128, 128), 128), :] = t.astype(bf16)


def cell_of(cell):
    cx, cy, z = cell // 128, (cell // 64) % 2, cell % 64
    return [((cx + dx) * 4 + cy + 1 + dy) * ZP + 1 + z + dz for dx, dy, dz in OFFS]


def make_d(cell, d_ref, a_ref, b_ref):
    a = a_ref[pl.ds(pl.multiple_of(cell * 128, 128), 128), :]
    zero = jnp.zeros((16, 128), bf16)
    ri = lax.broadcasted_iota(jnp.int32, (16, 128), 0)
    pick = jnp.where((ri >= 9) & (ri < 12), 1.0, 0.0).astype(bf16)
    ws = []
    for (dx, dy, dz), c in zip(OFFS, cell_of(cell)):
        b = b_ref[pl.ds(pl.multiple_of(c * 32, 32), 32), :]
        ws.append(jnp.concatenate([b[:16]] + [b[16:] if k == dz else zero for k in (-1, 0, 1)], 0))
    ws.append(jnp.concatenate([zero, pick, zero, zero], 0))
    for t in range(0, NT + 1, 2):
        w = jnp.concatenate(ws[t:t + 2], 1)
        d_ref[:, 128 * t:128 * t + w.shape[1]] = jnp.dot(a, w, preferred_element_type=f32)


def finish(cell, an_ref, as_ref, n_ref, s_ref):
    n_ref[pl.ds(cell, 1), :] = jnp.sum(an_ref[...].T, axis=0, keepdims=True)
    s_ref[pl.ds(cell, 1), :] = jnp.sum(as_ref[...].T, axis=0, keepdims=True)


def pair_sums(R, cell, d_ref, an_ref, as_ref, f_ref, jn_ref, js_ref):
    if R == 0:
        return
    cs = cell_of(cell)
    fj = [jnp.broadcast_to(f_ref[pl.ds(c, 1), :], (8, 128)) for c in cs]
    f0 = fj[0]
    for v in fj[1:]:
        f0 = f0 + v
    cn = [jnp.full((8, 128), -(R // 8.0), f32) for _ in cs]
    fi0 = d_ref[0:8, 128 * NT:128 * NT + 128]
    for r in range(8, R, 8):
        fi0 = fi0 + d_ref[r:r + 8, 128 * NT:128 * NT + 128]
    cm = [-fi0 for _ in cs]
    for r in range(0, R, 8):
        fi = d_ref[r:r + 8, 128 * NT:128 * NT + 128]
        an = jnp.full((8, 128), -float(NT), f32)
        am = -f0
        for t in range(NT):
            d = d_ref[r:r + 8, 128 * t:128 * t + 128]
            q = jnp.maximum(lax.rsqrt(jnp.maximum(d, 0.01)), 1.0)
            an = an + q
            am = am + q * fj[t]
            if t:
                cn[t] = cn[t] + q
                cm[t] = cm[t] + q * fi
        an_ref[r:r + 8, :] = an
        as_ref[r:r + 8, :] = am
    rows = [pl.ds(pl.multiple_of(c * 8, 8), 8) for c in cs]
    olds = [(jn_ref[rows[t], :], js_ref[rows[t], :]) for t in range(1, NT)]
    for t in range(1, NT):
        jn_ref[rows[t], :] = olds[t - 1][0] + cn[t]
        js_ref[rows[t], :] = olds[t - 1][1] + cm[t]


def tree(v, lo, hi, run):
    if hi - lo == 1:
        run(lo)
        return
    mid = (lo + hi) // 2

    @pl.when(v < mid)
    def _():
        tree(v, lo, mid, run)

    @pl.when(v >= mid)
    def _():
        tree(v, mid, hi, run)


def kern(MODE, sc_ref, cnt_ref, home, hy, hm, hx, hxp, hxm, n_ref, s_ref, hs_ref,
         a_ref, b_ref, f_ref, jn_ref, js_ref, stage, stage_a, d0, d1, an0, as0, an1, as1):
    x0 = sc_ref[0]
    y0 = sc_ref[1]
    stage[...] = jnp.zeros_like(stage)
    stage_a[...] = jnp.zeros_like(stage_a)
    ri = lax.broadcasted_iota(jnp.int32, (32, 128), 0)
    rim = (jnp.where(ri == 12, SENT * SENT, 0.0) + jnp.where((ri >= 22) & (ri < 25), 1.0, 0.0)).astype(bf16)

    @pl.loop(0, 12)
    def _(col):
        for zz in (0, ZP - 1):
            b_ref[pl.ds(pl.multiple_of((col * ZP + zz) * 32, 32), 32), :] = rim
            f_ref[pl.ds(col * ZP + zz, 1), :] = jnp.zeros((1, 128), f32)

    @pl.loop(0, 12 * ZP)
    def _(k):
        rows = pl.ds(pl.multiple_of(k * 8, 8), 8)
        jn_ref[rows, :] = jnp.zeros((8, 128), f32)
        js_ref[rows, :] = jnp.zeros((8, 128), f32)

    b = functools.partial(build_cols, x0=x0, y0=y0, b_ref=b_ref, f_ref=f_ref, a_ref=a_ref, stage=stage, stage_a=stage_a)

    @pl.loop(0, 4)
    def _(k):
        b(home, k * 64, (k // 2) * 4 + k % 2 + 1, own_cell=k * 64)

    @pl.loop(0, 2)
    def _(k):
        b(hy, k * 64, k * 4 + 3, own_cell=None)
        b(hx, k * 64, 9 + k, own_cell=None)
    b(hm, 0, 4, own_cell=None)
    b(hxp, 0, 11, own_cell=None)
    b(hxm, 0, 8, own_cell=None)

    if MODE == "build":
        n_ref[...] = jnp.zeros_like(n_ref)
        s_ref[...] = jnp.zeros_like(s_ref)
        hs_ref[...] = jnp.zeros_like(hs_ref)
        return
    make_d(0, d0, a_ref, b_ref)
    bufs = ((d0, an0, as0), (d1, an1, as1))

    @pl.loop(0, 128)
    def _(i):
        for p in range(2):
            cell = i * 2 + p
            nxt = jnp.minimum(cell + 1, 255)
            prev = jnp.maximum(cell - 1, 0)
            d, an, am = bufs[p]
            dn, anp, amp = bufs[1 - p]

            def run(k):
                if MODE != "nod":
                    make_d(nxt, dn, a_ref, b_ref)
                if MODE != "nofin":
                    finish(prev, anp, amp, n_ref, s_ref)
                if MODE != "nopair":
                    pair_sums(16 * k, cell, d, an, am, f_ref, jn_ref, js_ref)
            tree((cnt_ref[cell] + 15) // 16, 0, 9, run)
    finish(255, an1, as1, n_ref, s_ref)

    def side(col, z0, ref):
        base = (col * ZP + 1 + z0) * 8
        v = ref[pl.ds(base, 8, stride=8), :]
        for k in range(1, 8):
            v = v + ref[pl.ds(base + k, 8, stride=8), :]
        return v

    @pl.loop(0, 32)
    def _(k):
        cx, cy, z0 = k // 16, (k // 8) % 2, (k % 8) * 8
        rows = pl.ds(pl.multiple_of(k * 8, 8), 8)
        n_ref[rows, :] += side(cx * 4 + cy + 1, z0, jn_ref)
        s_ref[rows, :] += side(cx * 4 + cy + 1, z0, js_ref)

    @pl.loop(0, 8)
    def _(k):
        for h, col in enumerate((3, 7, 4, 9, 10, 11, 8)):
            rows = pl.ds(pl.multiple_of(h * 64 + k * 8, 8), 8)
            hs_ref[rows, 0:128] = side(col, k * 8, jn_ref)
            hs_ref[rows, 128:256] = side(col, k * 8, js_ref)


def compute(sc, cnt, home, hy, hm, hx, hxp, hxm, MODE="full"):
    vm = pl.BlockSpec(memory_space=pltpu.VMEM)
    sm = pl.BlockSpec(memory_space=pltpu.SMEM)
    return pl.pallas_call(
        functools.partial(kern, MODE),
        out_shape=[jax.ShapeDtypeStruct((256, 128), f32)] * 2 + [jax.ShapeDtypeStruct((448, 256), f32)],
        in_specs=[sm, sm] + [vm] * 6, out_specs=[vm] * 3,
        scratch_shapes=[pltpu.VMEM((256 * 128, 64), bf16), pltpu.VMEM((12 * ZP * 32, 128), bf16),
                        pltpu.VMEM((12 * ZP, 128), f32), pltpu.VMEM((12 * ZP * 8, 128), f32), pltpu.VMEM((12 * ZP * 8, 128), f32),
                        pltpu.VMEM((256, 128), f32), pltpu.VMEM((512, 128), f32)]
        + [pltpu.VMEM((128, 128 * (NT + 1)), f32)] * 2 + [pltpu.VMEM((128, 128), f32)] * 4,
        compiler_params=pltpu.CompilerParams(vmem_limit_bytes=56 * 2**20),
        name="pairs",
    )(sc, cnt, home, hy, hm, hx, hxp, hxm)


def turned(value, axes, step):
    size = (lax.axis_size("slab"), lax.axis_size("dom"))
    if len(axes) == 1:
        count = lax.axis_size(axes[0])
        return lax.ppermute(value, axes[0], [(i, (i + step[0]) % count) for i in range(count)])
    pairs = []
    for s in range(size[0]):
        for d in range(size[1]):
            pairs.append((s * size[1] + d, (s + step[0]) % size[0] * size[1] + (d + step[1]) % size[1]))
    return lax.ppermute(value, axes, pairs)


def local(incoming, dest, counts):
    cells = 256
    blocks = incoming.reshape(cells, 512)
    targets = dest.reshape(cells)
    me = lax.axis_index("dom")
    shift = (targets // cells - me + 2) % 32
    chosen = (shift[None, :] == jnp.arange(5)[:, None]).astype(f32)
    lower = (jnp.arange(cells)[:, None] <= jnp.arange(cells)[None, :]).astype(f32)
    rank = jnp.sum(jnp.dot(chosen, lower) * chosen, 0) - 1.0
    slot = shift.astype(f32) * 64.0 + rank
    pack = (jnp.arange(320, dtype=f32)[:, None] == slot[None, :]).astype(f32)
    tag = jnp.broadcast_to((targets % cells + 1).astype(f32)[:, None], (cells, 128))
    packed = jnp.dot(pack, jnp.concatenate([blocks, tag], 1), precision=lax.Precision.HIGHEST)
    got = [turned(packed[64 * k:64 * k + 64], ("dom",), (k - 2,)) if k != 2 else packed[128:192] for k in range(5)]
    got = jnp.concatenate(got, 0)
    place = (jnp.arange(cells, dtype=f32)[:, None] + 1.0 == got[None, :, 512]).astype(f32)
    home = jnp.dot(place, got[:, :512], precision=lax.Precision.HIGHEST)
    count = counts.reshape(cells)
    filled = jnp.arange(128)[None, :] < count[:, None]
    x0 = (lax.axis_index("slab") * 2 + 1).astype(f32)
    y0 = (me * 2 + 1).astype(f32)
    home = jnp.concatenate(
        [jnp.where(filled, home[:, :128], x0 + SENT), home[:, 128:384], jnp.where(filled, home[:, 384:], 0.0)], 1)
    both = ("slab", "dom")
    hy = turned(jnp.concatenate([home[0:64], home[128:192]], 0), ("dom",), (-1,))
    hm = turned(home[192:256], ("dom",), (1,))
    hx = turned(home[0:128], ("slab",), (-1,))
    hxp = turned(home[0:64], both, (-1, -1))
    hxm = turned(home[64:128], both, (-1, 1))
    n, s, hs = compute(jnp.stack([x0, y0]), count, home, hy, hm, hx, hxp, hxm)
    by = turned(hs[0:128], ("dom",), (1,))
    bm = turned(hs[128:192], ("dom",), (-1,))
    bx = turned(hs[192:320], ("slab",), (1,))
    bxp = turned(hs[320:384], both, (1, 1))
    bxm = turned(hs[384:448], both, (1, -1))
    back = jnp.concatenate([by[:64] + bx[:64] + bxp, bx[64:] + bxm, by[64:], bm], 0)
    n = n + back[:, :128]
    s = s + back[:, 128:]
    own = lax.rsqrt(jnp.full((), 0.01, f32)) - 1.0
    density = jnp.where(filled, (n - own) / ref_density, 0.0)
    laplace = jnp.where(filled, (s - home[:, 384:] * n) / ref_density, 0.0)
    return density.reshape(2, 2, 64, 128), laplace.reshape(2, 2, 64, 128)


def solution(mesh):
    in_specs = (P("slab", "dom", None, None), P("slab", "dom"), P("slab", "dom", None))
    out_specs = (P("slab", "dom", None, None), P("slab", "dom", None, None))
    return jax.shard_map(local, mesh=mesh, in_specs=in_specs, out_specs=out_specs, check_vma=False)
```

time: 658 us -> 206 us (0.31)
  other arithmetic: 367 us -> 1.66 us
  local copies, waits for them, and re-layouts: 218 us -> 7.92 us
  Pallas kernels: 0 us -> 147 us
  starting transfers between devices: 46.4 us -> 20.6 us
    reduce_sum x28 -> x0, other arithmetic: 347 us -> none  [one_block(): (weight * own_part[:, 3, :, None]).sum(1)]
    pallas_call x0 -> x1, Pallas kernels: none -> 147 us  [compute(): pl.pallas_call(functools.partial(kern, MODE), out_shape=[jax.ShapeDtypeSt...]
    dynamic_update_slice x216 -> x0, local copies, waits for them, and re-layouts: 131 us -> none  [shell_sums(): lax.map(one_block, (split_rows(own_cells), split_rows(own_mask), far_stac...]
    ppermute x20 -> x14, starting transfers between devices: 46.4 us -> 20.6 us  [the longest x10 18.3 us: turned(): lax.ppermute(value, axes[0], [(i, (i + step[0]) % count) for i in range(c...]
    squeeze x34 -> x0, local copies, waits for them, and re-layouts: 19.7 us -> none  [the longest x28 19.7 us: shell_sums(): lax.map(one_block, (split_rows(own_cells), split_rows(own_mask), far_stac...]
    mul x80 -> x0, local copies, waits for them, and re-layouts: 19.4 us -> none  [the longest x28 18.8 us: pair_weights(): jnp.maximum(radius_eff / radius - 1.0, 0.0) * own_mask[:, :, None]]
    scatter-add x49 -> x0, local copies, waits for them, and re-layouts: 17.6 us -> none  [the longest x14 4.95 us: local(): sum_n.at[start_x:start_x + cells_x, 1:1 + cells_y, 1:1 + cells_z]]
    scatter x9 -> x0, local copies, waits for them, and re-layouts: 14.3 us -> none  [the longest x4 6.41 us: local(): jnp.zeros((capacity + 1, channels), jnp.float32).at[slot_ids].set(blocks)]
  transfers between devices with their start and end apart: 20 -> 14, of which waited for: 6 -> 9; matrix products, arithmetic and copies ran while one was open for 5% -> 1% of each run, Pallas kernels for 0% -> 0%
where the time goes in v1:
time: 206 us; the launch traced here: 205 us
  Pallas kernels  147 us (71%)
  waiting for transfers between devices  25 us (12%)
  starting transfers between devices  20.6 us (10%)
  local copies, waits for them, and re-layouts  7.92 us (4%)
    pallas_call x1, Pallas kernels, compute(): pl.pallas_call(functools.partial(kern, MODE), out_shape=[jax.ShapeDtypeSt...  147 us
    ppermute x10, starting transfers between devices, turned(): lax.ppermute(value, axes[0], [(i, (i + step[0]) % count) for i in range(c...  18.3 us
    ppermute x10, waiting for transfers between devices, turned(): lax.ppermute(value, axes[0], [(i, (i + step[0]) % count) for i in range(c...  15.9 us
    ppermute x4, waiting for transfers between devices, turned(): return lax.ppermute(value, axes, pairs)  9.16 us
    unnamed x28, local copies, waits for them, and re-layouts  5.56 us
  transfers between devices with their start and end apart: 14, of which 9 were waited for; matrix products, arithmetic and copies ran while one was open for 1% of the time, Pallas kernels for 0%

profile of v1, /device:TPU:1, one launch (start us, length us, event | category | flops | bytes accessed | tf_op | source)
XLA Modules:
  0.0 204.6 jit_solution(16492781829509652839)
XLA Ops:
  0.6 0.7 copy-done.10
  1.5 1.1 copy.7
  2.7 0.7 fusion.3
  3.4 7.1 %collective-permute-start = (f32[64,640]{1,0:T(8,128)S(1)}, f32[64,640]{1,0:T(8,128)S(1)}, u32[]{:S(2)}, u32[]{:S(2)}) collective-permute-start(f32[64,640]{1,0:T(8,128)S(1)} %get-tuple-element.12), channel_id=1, source_target_pairs={{0,30},{1,31},{2,0},{3,1},{4,2},{5,3},{6,4},{7,5},{8,6},{9,7},{10,... | collective-permute-start | bytes 491528 | tf_op jit(solution)/shard_map/ppermute | solution.py:244
  10.5 1.0 collective-permute-start.1
  11.5 1.9 collective-permute-done
  13.4 1.9 collective-permute-done.1
  15.5 0.7 copy-done.11
  16.3 1.4 collective-permute-done.2
  17.7 10.1 %collective-permute-done.3 = f32[64,640]{1,0:T(8,128)S(1)} collective-permute-done((f32[64,640]{1,0:T(8,128)S(1)}, f32[64,640]{1,0:T(8,128)S(1)}, u32[]{:S(2)}, u32[]{:S(2)}) %collective-permute-start.3) | collective-permute-done | bytes 163872 | tf_op jit(solution)/shard_map/ppermute | solution.py:244
  28.1 0.7 fusion.1
  29.0 0.8 copy-done
  29.9 2.6 %collective-permute-start.6 = (f32[128,512]{1,0:T(8,128)S(1)}, f32[128,512]{1,0:T(8,128)S(1)}, u32[]{:S(2)}, u32[]{:S(2)}) collective-permute-start(f32[128,512]{1,0:T(8,128)S(1)} %slice.118), channel_id=1, source_target_pairs={{0,96},{32,0},{64,32},{96,64},{1,97},{33,1},{65,33},{97,65},{2,98}... | collective-permute-start | bytes 786440 | tf_op jit(solution)/shard_map/ppermute | solution.py:244
  32.4 1.2 collective-permute-start.7
  33.6 0.8 collective-permute-start.5
  34.4 0.8 collective-permute-start.8
  35.3 0.6 pad_maximum_fusion.3.sc_ref
  35.9 0.5 collective-permute-done.5.hm
  36.4 4.4 %collective-permute-done.7.hxp = f32[64,512]{1,0:T(8,128)S(1)} collective-permute-done((f32[64,512]{1,0:T(8,128)S(1)}, f32[64,512]{1,0:T(8,128)S(1)}, u32[]{:S(2)}, u32[]{:S(2)}) %collective-permute-start.7) | collective-permute-done | bytes 131104 | tf_op jit(solution)/shard_map/ppermute | solution.py:249
  40.8 3.1 %collective-permute-done.8.hxm = f32[64,512]{1,0:T(8,128)S(1)} collective-permute-done((f32[64,512]{1,0:T(8,128)S(1)}, f32[64,512]{1,0:T(8,128)S(1)}, u32[]{:S(2)}, u32[]{:S(2)}) %collective-permute-start.8) | collective-permute-done | bytes 131104 | tf_op jit(solution)/shard_map/ppermute | solution.py:249
  43.9 0.6 copy-done.5
  44.6 0.7 copy-done.2
  45.3 147.0 %pairs.1 = (f32[256,128]{1,0:T(8,128)}, f32[256,128]{1,0:T(8,128)}, f32[448,256]{1,0:T(8,128)}) custom-call(f32[2]{0:T(128)} %pad_maximum_fusion.3.sc_ref, s32[256]{0:T(256)} %copy-done.8, f32[256,512]{1,0:T(8,128)} %copy-done, f32[128,512]{1,0:T(8,128)} %copy-done.1, f32[64,512]{1,0:T(8,128)} %copy-done.4, f32[128,512]{1,0:T(8,128)} %copy-done.2, ...), custom_call_target="tpu_custom_call" | custom-call | tf_op jit(solution)/shard_map/pairs/pallas_call | solution.py:227
  192.3 1.0 fusion.25
  193.3 1.6 collective-permute-start.10
  194.9 0.4 collective-permute-start.9
  195.3 0.9 fusion.24
  196.5 4.7 %collective-permute-start.13 = (f32[64,256]{1,0:T(8,128)S(1)}, f32[64,256]{1,0:T(8,128)S(1)}, u32[]{:S(2)}, u32[]{:S(2)}) collective-permute-start(f32[64,256]{1,0:T(8,128)S(1)} %get-tuple-element.20), channel_id=1, source_target_pairs={{0,31},{1,0},{2,1},{3,2},{4,3},{5,4},{6,5},{7,6},{8,7},{9,8},{10,9... | collective-permute-start | bytes 196616 | tf_op jit(solution)/shard_map/ppermute | solution.py:244
  201.1 1.0 collective-permute-done.11
  202.1 0.6 collective-permute-done.12
  202.9 0.8 copy-done.6
  203.8 0.8 fusion.13
  (51 shorter events, 1.6 us)
Async XLA Ops:
  0.6 0.7 copy-start.10
  3.4 10.0 %collective-permute-start = (f32[64,640]{1,0:T(8,128)S(1)}, f32[64,640]{1,0:T(8,128)S(1)}, u32[]{:S(2)}, u32[]{:S(2)}) collective-permute-start(f32[64,640]{1,0:T(8,128)S(1)} %get-tuple-element.12), channel_id=1, source_target_pairs={{0,30},{1,31},{2,0},{3,1},{4,2},{5,3},{6,4},{7,5},{8,6},{9,7},{10,... | collective-permute-start | bytes 491528 | tf_op jit(solution)/shard_map/ppermute | solution.py:244
  10.5 4.7 %collective-permute-start.1 = (f32[64,640]{1,0:T(8,128)S(1)}, f32[64,640]{1,0:T(8,128)S(1)}, u32[]{:S(2)}, u32[]{:S(2)}) collective-permute-start(f32[64,640]{1,0:T(8,128)S(1)} %get-tuple-element.11), channel_id=1, source_target_pairs={{0,31},{1,0},{2,1},{3,2},{4,3},{5,4},{6,5},{7,6},{8,7},{9,8},{10,9... | collective-permute-start | bytes 491528 | tf_op jit(solution)/shard_map/ppermute | solution.py:244
  15.3 2.4 %collective-permute-start.2 = (f32[64,640]{1,0:T(8,128)S(1)}, f32[64,640]{1,0:T(8,128)S(1)}, u32[]{:S(2)}, u32[]{:S(2)}) collective-permute-start(f32[64,640]{1,0:T(8,128)S(1)} %get-tuple-element.9), channel_id=1, source_target_pairs={{0,1},{1,2},{2,3},{3,4},{4,5},{5,6},{6,7},{7,8},{8,9},{9,10},{10,1... | collective-permute-start | bytes 491528 | tf_op jit(solution)/shard_map/ppermute | solution.py:244
  15.4 12.5 %collective-permute-start.3 = (f32[64,640]{1,0:T(8,128)S(1)}, f32[64,640]{1,0:T(8,128)S(1)}, u32[]{:S(2)}, u32[]{:S(2)}) collective-permute-start(f32[64,640]{1,0:T(8,128)S(1)} %get-tuple-element.8), channel_id=1, source_target_pairs={{0,2},{1,3},{2,4},{3,5},{4,6},{5,7},{6,8},{7,9},{8,10},{9,11},{10,... | collective-permute-start | bytes 491528 | tf_op jit(solution)/shard_map/ppermute | solution.py:244
  15.5 0.7 copy-start.11
  16.3 12.4 %copy-start.8 = (s32[256]{0:T(256)}, s32[256]{0:T(256)S(1)}, u32[]{:S(2)}) copy-start(s32[256]{0:T(256)S(1)} %lt.26.cnt_ref) | copy-start | bytes 3076
  28.9 0.8 copy-start
  29.8 14.1 %collective-permute-start.4 = (f32[128,512]{1,0:T(8,128)S(1)}, f32[128,512]{1,0:T(8,128)S(1)}, u32[]{:S(2)}, u32[]{:S(2)}) collective-permute-start(f32[128,512]{1,0:T(8,128)S(1)} %pad_maximum_fusion.1), channel_id=1, source_target_pairs={{0,31},{1,0},{2,1},{3,2},{4,3},{5,4},{6,5},{7,6},{8,7},{9,8},{10,9... | collective-permute-start | bytes 786440 | tf_op jit(solution)/shard_map/ppermute | solution.py:244
  29.9 14.0 %collective-permute-start.6 = (f32[128,512]{1,0:T(8,128)S(1)}, f32[128,512]{1,0:T(8,128)S(1)}, u32[]{:S(2)}, u32[]{:S(2)}) collective-permute-start(f32[128,512]{1,0:T(8,128)S(1)} %slice.118), channel_id=1, source_target_pairs={{0,96},{32,0},{64,32},{96,64},{1,97},{33,1},{65,33},{97,65},{2,98}... | collective-permute-start | bytes 786440 | tf_op jit(solution)/shard_map/ppermute | solution.py:244
  32.4 8.3 %collective-permute-start.7 = (f32[64,512]{1,0:T(8,128)S(1)}, f32[64,512]{1,0:T(8,128)S(1)}, u32[]{:S(2)}, u32[]{:S(2)}) collective-permute-start(f32[64,512]{1,0:T(8,128)S(1)} %get-tuple-element.18), channel_id=1, source_target_pairs={{0,127},{1,96},{2,97},{3,98},{4,99},{5,100},{6,101},{7,102},{8,103... | collective-permute-start | bytes 393224 | tf_op jit(solution)/shard_map/ppermute | solution.py:249
  33.6 2.8 %collective-permute-start.5 = (f32[64,512]{1,0:T(8,128)S(1)}, f32[64,512]{1,0:T(8,128)S(1)}, u32[]{:S(2)}, u32[]{:S(2)}) collective-permute-start(f32[64,512]{1,0:T(8,128)S(1)} %get-tuple-element.16), channel_id=1, source_target_pairs={{0,1},{1,2},{2,3},{3,4},{4,5},{5,6},{6,7},{7,8},{8,9},{9,10},{10,1... | collective-permute-start | bytes 393224 | tf_op jit(solution)/shard_map/ppermute | solution.py:244
  34.4 9.4 %collective-permute-start.8 = (f32[64,512]{1,0:T(8,128)S(1)}, f32[64,512]{1,0:T(8,128)S(1)}, u32[]{:S(2)}, u32[]{:S(2)}) collective-permute-start(f32[64,512]{1,0:T(8,128)S(1)} %get-tuple-element.15), channel_id=1, source_target_pairs={{0,97},{1,98},{2,99},{3,100},{4,101},{5,102},{6,103},{7,104},{8,10... | collective-permute-start | bytes 393224 | tf_op jit(solution)/shard_map/ppermute | solution.py:249
  36.4 7.5 %copy-start.4 = (f32[64,512]{1,0:T(8,128)}, f32[64,512]{1,0:T(8,128)S(1)}, u32[]{:S(2)}) copy-start(f32[64,512]{1,0:T(8,128)S(1)} %collective-permute-done.5.hm) | copy-start | bytes 393220
  40.8 3.1 %copy-start.3 = (f32[64,512]{1,0:T(8,128)}, f32[64,512]{1,0:T(8,128)S(1)}, u32[]{:S(2)}) copy-start(f32[64,512]{1,0:T(8,128)S(1)} %collective-permute-done.7.hxp) | copy-start | bytes 393220
  43.9 0.6 copy-start.5
  43.9 0.7 copy-start.1
  44.6 0.7 copy-start.2
  193.3 9.5 %collective-permute-start.10 = (f32[128,256]{1,0:T(8,128)S(1)}, f32[128,256]{1,0:T(8,128)S(1)}, u32[]{:S(2)}, u32[]{:S(2)}) collective-permute-start(f32[128,256]{1,0:T(8,128)S(1)} %get-tuple-element.22), channel_id=1, source_target_pairs={{0,32},{32,64},{64,96},{96,0},{1,33},{33,65},{65,97},{97,1},{2,34}... | collective-permute-start | bytes 393224 | tf_op jit(solution)/shard_map/ppermute | solution.py:244
  194.9 7.9 %collective-permute-start.9 = (f32[128,256]{1,0:T(8,128)S(1)}, f32[128,256]{1,0:T(8,128)S(1)}, u32[]{:S(2)}, u32[]{:S(2)}) collective-permute-start(f32[128,256]{1,0:T(8,128)S(1)} %get-tuple-element.23), channel_id=1, source_target_pairs={{0,1},{1,2},{2,3},{3,4},{4,5},{5,6},{6,7},{7,8},{8,9},{9,10},{10,1... | collective-permute-start | bytes 393224 | tf_op jit(solution)/shard_map/ppermute | solution.py:244
  196.2 5.9 %collective-permute-start.11 = (f32[64,256]{1,0:T(8,128)S(1)}, f32[64,256]{1,0:T(8,128)S(1)}, u32[]{:S(2)}, u32[]{:S(2)}) collective-permute-start(f32[64,256]{1,0:T(8,128)S(1)} %get-tuple-element.19), channel_id=1, source_target_pairs={{0,33},{1,34},{2,35},{3,36},{4,37},{5,38},{6,39},{7,40},{8,41},{9,... | collective-permute-start | bytes 196616 | tf_op jit(solution)/shard_map/ppermute | solution.py:249
  196.3 6.5 %collective-permute-start.12 = (f32[64,256]{1,0:T(8,128)S(1)}, f32[64,256]{1,0:T(8,128)S(1)}, u32[]{:S(2)}, u32[]{:S(2)}) collective-permute-start(f32[64,256]{1,0:T(8,128)S(1)} %get-tuple-element.21), channel_id=1, source_target_pairs={{0,63},{1,32},{2,33},{3,34},{4,35},{5,36},{6,37},{7,38},{8,39},{9,... | collective-permute-start | bytes 196616 | tf_op jit(solution)/shard_map/ppermute | solution.py:249
  196.5 6.4 %collective-permute-start.13 = (f32[64,256]{1,0:T(8,128)S(1)}, f32[64,256]{1,0:T(8,128)S(1)}, u32[]{:S(2)}, u32[]{:S(2)}) collective-permute-start(f32[64,256]{1,0:T(8,128)S(1)} %get-tuple-element.20), channel_id=1, source_target_pairs={{0,31},{1,0},{2,1},{3,2},{4,3},{5,4},{6,5},{7,6},{8,7},{9,8},{10,9... | collective-permute-start | bytes 196616 | tf_op jit(solution)/shard_map/ppermute | solution.py:244
  202.8 0.9 copy-start.6
  202.8 1.0 copy-start.7
  202.9 0.9 copy-start.9

commit v2 on v1

--- a/solution.py
+++ b/solution.py
@@ -9,9 +9,11 @@
 SENT = 100.0
 ZP = 66
 ref_density = 268.0825731
+N_SLAB, N_DOM = 4, 32
 
 OFFS = [(0, 0, 0), (0, 0, 1)] + [(dx, dy, dz) for dx, dy in ((0, 1), (1, -1), (1, 0), (1, 1)) for dz in (-1, 0, 1)]
 NT = len(OFFS)
+FR = 4
 
 
 def split3(v):
@@ -78,9 +80,11 @@
         b = b_ref[pl.ds(pl.multiple_of(c * 32, 32), 32), :]
         ws.append(jnp.concatenate([b[:16]] + [b[16:] if k == dz else zero for k in (-1, 0, 1)], 0))
     ws.append(jnp.concatenate([zero, pick, zero, zero], 0))
-    for t in range(0, NT + 1, 2):
+
+    def part(t):
         w = jnp.concatenate(ws[t:t + 2], 1)
         d_ref[:, 128 * t:128 * t + w.shape[1]] = jnp.dot(a, w, preferred_element_type=f32)
+    return [functools.partial(part, t) for t in range(0, NT + 1, 2)]
 
 
 def finish(cell, an_ref, as_ref, n_ref, s_ref):
@@ -88,8 +92,10 @@
     s_ref[pl.ds(cell, 1), :] = jnp.sum(as_ref[...].T, axis=0, keepdims=True)
 
 
-def pair_sums(R, cell, d_ref, an_ref, as_ref, f_ref, jn_ref, js_ref):
+def pair_sums(R, cell, d_ref, an_ref, as_ref, f_ref, jn_ref, js_ref, parts):
     if R == 0:
+        for part in parts:
+            part()
         return
     cs = cell_of(cell)
     fj = [jnp.broadcast_to(f_ref[pl.ds(c, 1), :], (8, 128)) for c in cs]
@@ -115,6 +121,8 @@
                 cm[t] = cm[t] + q * fi
         an_ref[r:r + 8, :] = an
         as_ref[r:r + 8, :] = am
+        for part in parts[min(FR * r * len(parts) // R // 4, len(parts)):min(FR * (r + 8) * len(parts) // R // 4, len(parts))]:
+            part()
     rows = [pl.ds(pl.multiple_of(c * 8, 8), 8) for c in cs]
     olds = [(jn_ref[rows[t], :], js_ref[rows[t], :]) for t in range(1, NT)]
     for t in range(1, NT):
@@ -177,7 +185,8 @@
         s_ref[...] = jnp.zeros_like(s_ref)
         hs_ref[...] = jnp.zeros_like(hs_ref)
         return
-    make_d(0, d0, a_ref, b_ref)
+    for part in make_d(0, d0, a_ref, b_ref):
+        part()
     bufs = ((d0, an0, as0), (d1, an1, as1))
 
     @pl.loop(0, 128)
@@ -190,12 +199,11 @@
             dn, anp, amp = bufs[1 - p]
 
             def run(k):
-                if MODE != "nod":
-                    make_d(nxt, dn, a_ref, b_ref)
+                parts = make_d(nxt, dn, a_ref, b_ref)
                 if MODE != "nofin":
                     finish(prev, anp, amp, n_ref, s_ref)
                 if MODE != "nopair":
-                    pair_sums(16 * k, cell, d, an, am, f_ref, jn_ref, js_ref)
+                    pair_sums(16 * k, cell, d, an, am, f_ref, jn_ref, js_ref, parts)
             tree((cnt_ref[cell] + 15) // 16, 0, 9, run)
     finish(255, an1, as1, n_ref, s_ref)
 
@@ -237,59 +245,158 @@
     )(sc, cnt, home, hy, hm, hx, hxp, hxm)
 
 
-def turned(value, axes, step):
-    size = (lax.axis_size("slab"), lax.axis_size("dom"))
-    if len(axes) == 1:
-        count = lax.axis_size(axes[0])
-        return lax.ppermute(value, axes[0], [(i, (i + step[0]) % count) for i in range(count)])
-    pairs = []
-    for s in range(size[0]):
-        for d in range(size[1]):
-            pairs.append((s * size[1] + d, (s + step[0]) % size[0] * size[1] + (d + step[1]) % size[1]))
-    return lax.ppermute(value, axes, pairs)
+def far(ds, dd):
+    slab = lax.rem(lax.axis_index("slab") + (ds + N_SLAB), N_SLAB)
+    dom = lax.rem(lax.axis_index("dom") + (dd + N_DOM), N_DOM)
+    return (slab, dom)
+
+
+def copy_to(src, dst, send, recv, where):
+    return pltpu.make_async_remote_copy(
+        src_ref=src, dst_ref=dst, send_sem=send, recv_sem=recv, device_id=far(*where),
+        device_id_type=pl.DeviceIdType.MESH)
+
+
+def greet(senders):
+    barrier = pltpu.get_barrier_semaphore()
+    for where in senders:
+        pl.semaphore_signal(barrier, inc=1, device_id=far(*where), device_id_type=pl.DeviceIdType.MESH)
+    pl.semaphore_wait(barrier, len(senders))
+
+
+def picked(onehot, v, dims):
+    out = None
+    for part in reversed(split3(v)):
+        p = lax.dot_general(onehot, part.astype(bf16), (dims, ((), ())), preferred_element_type=f32)
+        out = p if out is None else out + p
+    return out
+
+
+def iota(shape, dim):
+    return lax.broadcasted_iota(jnp.int32, shape, dim).astype(f32)
+
+
+FAR = (0, 4, 1, 3)
+HALO = ((0, 64, (0, -1), 0, 0), (128, 64, (0, -1), 0, 64), (192, 64, (0, 1), 1, 0), (0, 128, (-1, 0), 2, 0),
+        (0, 64, (-1, -1), 3, 0), (64, 64, (-1, 1), 4, 0))
+
+
+def relayout_kernel(x_ref, dest_ref, cnt_ref, home, hy, hm, hx, hxp, hxm, sent, got, s1, r1, s2, r2):
+    me = lax.axis_index("dom")
+    greet([(0, -2), (0, -1), (0, 1), (0, 2), (1, 0), (1, 1), (1, -1)])
+    dest = dest_ref[...]
+    dom = lax.shift_right_logical(dest, 8)
+    shift = (dom - me).astype(f32)
+    shift = jnp.where(shift < -16.0, shift + 32.0, jnp.where(shift > 16.0, shift - 32.0, shift)) + 2.0
+    local = (dest - dom * 256).astype(f32)
+    chosen = jnp.where(iota((8, 256), 0) == shift, 1.0, 0.0)
+    lower = jnp.where(iota((256, 256), 0) <= iota((256, 256), 1), 1.0, 0.0).astype(bf16)
+    rank = jnp.dot(chosen.astype(bf16), lower, preferred_element_type=f32)
+    rank = jnp.sum(chosen * rank, axis=0, keepdims=True) - 1.0
+    slot = shift * 64.0 + rank
+    xs = [x_ref[:, c, :] for c in range(4)]
+    diag = jnp.where(iota((256, 256), 0) == iota((256, 256), 1), 1.0, 0.0)
+    tag = jnp.broadcast_to(jnp.sum(diag * local, axis=1, keepdims=True) + 1.0, (256, 128))
+    data = jnp.concatenate(xs, 1)
+    first = []
+    for k in FAR:
+        pack = jnp.where(iota((64, 256), 0) + 64.0 * k == slot, 1.0, 0.0).astype(bf16)
+        sent[k, :, 0:512] = picked(pack, data, ((1,), (0,)))
+        sent[k, :, 512:640] = jnp.dot(pack, tag.astype(bf16), preferred_element_type=f32)
+        c = copy_to(sent.at[k], got.at[k], s1.at[k], r1.at[k], (0, k - 2))
+        c.start()
+        first.append(c)
+    pack = jnp.where(iota((64, 256), 0) + 128.0 == slot, 1.0, 0.0).astype(bf16)
+    got[2, :, 0:512] = picked(pack, data, ((1,), (0,)))
+    got[2, :, 512:640] = jnp.dot(pack, tag.astype(bf16), preferred_element_type=f32)
+    count = jnp.sum(diag * cnt_ref[...].astype(f32), axis=1, keepdims=True)
+    filled = iota((256, 128), 1) < count
+    total = None
+    for k in (2,) + FAR[::-1]:
+        if k != 2:
+            first[FAR.index(k)].wait_recv()
+        label = got[k, :, 512:640]
+        lanes = iota((64, 128), 1)
+        place = jnp.concatenate([jnp.where(label == lanes + 1.0, 1.0, 0.0), jnp.where(label == lanes + 129.0, 1.0, 0.0)], 1)
+        part = picked(place.T.astype(bf16), got[k, :, 0:512], ((1,), (0,)))
+        total = part if total is None else total + part
+    x0 = (lax.axis_index("slab") * 2 + 1).astype(f32)
+    home[:, 0:128] = jnp.where(filled, total[:, 0:128], x0 + SENT)
+    home[:, 128:384] = total[:, 128:384]
+    home[:, 384:512] = jnp.where(filled, total[:, 384:512], 0.0)
+    outs = (hy, hm, hx, hxp, hxm)
+    second = []
+    for k, (row, rows, where, o, there) in enumerate(HALO):
+        c = copy_to(home.at[pl.ds(row, rows)], outs[o].at[pl.ds(there, rows)], s2.at[k], r2.at[k], where)
+        c.start()
+        second.append(c)
+    for c in first:
+        c.wait_send()
+    for c in second:
+        c.wait()
+
+
+def relayout(x, dest, count):
+    vm = pl.BlockSpec(memory_space=pltpu.VMEM)
+    return pl.pallas_call(
+        relayout_kernel,
+        out_shape=[jax.ShapeDtypeStruct((r, 512), f32) for r in (256, 128, 64, 128, 64, 64)],
+        in_specs=[vm] * 3, out_specs=[vm] * 6,
+        scratch_shapes=[pltpu.VMEM((5, 64, 640), f32)] * 2
+        + [pltpu.SemaphoreType.DMA((5,))] * 2 + [pltpu.SemaphoreType.DMA((6,))] * 2,
+        compiler_params=pltpu.CompilerParams(collective_id=0, has_side_effects=True, vmem_limit_bytes=32 * 2**20),
+        name="relayout",
+    )(x, dest, count)
+
+
+BACK = ((0, 128, (0, 1)), (128, 64, (0, -1)), (192, 128, (1, 0)), (320, 64, (1, 1)), (384, 64, (1, -1)))
+
+
+def combine_kernel(n_ref, s_ref, hs, home, cnt_ref, dens, lap, got, s1, r1):
+    greet([(0, -1), (0, 1), (-1, 0), (-1, -1), (-1, 1)])
+    copies = []
+    for k, (row, rows, where) in enumerate(BACK):
+        part = pl.ds(row, rows)
+        c = copy_to(hs.at[part], got.at[part], s1.at[k], r1.at[k], where)
+        c.start()
+        copies.append(c)
+    diag = jnp.where(iota((256, 256), 0) == iota((256, 256), 1), 1.0, 0.0)
+    count = jnp.sum(diag * cnt_ref[...].astype(f32), axis=1, keepdims=True)
+    for c in copies:
+        c.wait()
+    own = lax.rsqrt(jnp.full((64, 128), 0.01, f32)) - 1.0
+    lists = ((0, 192, 320), (256, 384), (64,), (128,))
+    for q in range(4):
+        rows = slice(64 * q, 64 * q + 64)
+        n = n_ref[rows, :]
+        s = s_ref[rows, :]
+        for r in lists[q]:
+            n = n + got[r:r + 64, 0:128]
+            s = s + got[r:r + 64, 128:256]
+        filled = iota((64, 128), 1) < count[rows]
+        dens[rows, :] = jnp.where(filled, (n - own) / ref_density, 0.0)
+        lap[rows, :] = jnp.where(filled, (s - home[rows, 384:512] * n) / ref_density, 0.0)
+
+
+def combine(n, s, hs, home, count):
+    vm = pl.BlockSpec(memory_space=pltpu.VMEM)
+    return pl.pallas_call(
+        combine_kernel,
+        out_shape=[jax.ShapeDtypeStruct((256, 128), f32)] * 2,
+        in_specs=[vm] * 5, out_specs=[vm] * 2,
+        scratch_shapes=[pltpu.VMEM((448, 256), f32), pltpu.SemaphoreType.DMA((5,)), pltpu.SemaphoreType.DMA((5,))],
+        compiler_params=pltpu.CompilerParams(collective_id=1, has_side_effects=True, vmem_limit_bytes=16 * 2**20),
+        name="combine",
+    )(n, s, hs, home, count)
 
 
 def local(incoming, dest, counts):
-    cells = 256
-    blocks = incoming.reshape(cells, 512)
-    targets = dest.reshape(cells)
-    me = lax.axis_index("dom")
-    shift = (targets // cells - me + 2) % 32
-    chosen = (shift[None, :] == jnp.arange(5)[:, None]).astype(f32)
-    lower = (jnp.arange(cells)[:, None] <= jnp.arange(cells)[None, :]).astype(f32)
-    rank = jnp.sum(jnp.dot(chosen, lower) * chosen, 0) - 1.0
-    slot = shift.astype(f32) * 64.0 + rank
-    pack = (jnp.arange(320, dtype=f32)[:, None] == slot[None, :]).astype(f32)
-    tag = jnp.broadcast_to((targets % cells + 1).astype(f32)[:, None], (cells, 128))
-    packed = jnp.dot(pack, jnp.concatenate([blocks, tag], 1), precision=lax.Precision.HIGHEST)
-    got = [turned(packed[64 * k:64 * k + 64], ("dom",), (k - 2,)) if k != 2 else packed[128:192] for k in range(5)]
-    got = jnp.concatenate(got, 0)
-    place = (jnp.arange(cells, dtype=f32)[:, None] + 1.0 == got[None, :, 512]).astype(f32)
-    home = jnp.dot(place, got[:, :512], precision=lax.Precision.HIGHEST)
-    count = counts.reshape(cells)
-    filled = jnp.arange(128)[None, :] < count[:, None]
+    count = counts.reshape(256)
     x0 = (lax.axis_index("slab") * 2 + 1).astype(f32)
-    y0 = (me * 2 + 1).astype(f32)
-    home = jnp.concatenate(
-        [jnp.where(filled, home[:, :128], x0 + SENT), home[:, 128:384], jnp.where(filled, home[:, 384:], 0.0)], 1)
-    both = ("slab", "dom")
-    hy = turned(jnp.concatenate([home[0:64], home[128:192]], 0), ("dom",), (-1,))
-    hm = turned(home[192:256], ("dom",), (1,))
-    hx = turned(home[0:128], ("slab",), (-1,))
-    hxp = turned(home[0:64], both, (-1, -1))
-    hxm = turned(home[64:128], both, (-1, 1))
+    y0 = (lax.axis_index("dom") * 2 + 1).astype(f32)
+    home, hy, hm, hx, hxp, hxm = relayout(incoming.reshape(256, 4, 128), dest, count.reshape(1, 256))
     n, s, hs = compute(jnp.stack([x0, y0]), count, home, hy, hm, hx, hxp, hxm)
-    by = turned(hs[0:128], ("dom",), (1,))
-    bm = turned(hs[128:192], ("dom",), (-1,))
-    bx = turned(hs[192:320], ("slab",), (1,))
-    bxp = turned(hs[320:384], both, (1, 1))
-    bxm = turned(hs[384:448], both, (1, -1))
-    back = jnp.concatenate([by[:64] + bx[:64] + bxp, bx[64:] + bxm, by[64:], bm], 0)
-    n = n + back[:, :128]
-    s = s + back[:, 128:]
-    own = lax.rsqrt(jnp.full((), 0.01, f32)) - 1.0
-    density = jnp.where(filled, (n - own) / ref_density, 0.0)
-    laplace = jnp.where(filled, (s - home[:, 384:] * n) / ref_density, 0.0)
+    density, laplace = combine(n, s, hs, home, count.reshape(1, 256))
     return density.reshape(2, 2, 64, 128), laplace.reshape(2, 2, 64, 128)
 
 

time: 206 us -> 167 us (0.81)
  waiting for transfers between devices: 25 us -> 0 us
  starting transfers between devices: 20.6 us -> 0 us
  Pallas kernels: 147 us -> 155 us
  local copies, waits for them, and re-layouts: 7.92 us -> 10.2 us
    pallas_call x0 -> x2, Pallas kernels: none -> 40.8 us  [the longest x1 27.2 us: relayout(): pl.pallas_call(relayout_kernel, out_shape=[jax.ShapeDtypeStruct((r, 512),...]
    pallas_call x1, Pallas kernels: 147 us -> 114 us  [compute(): pl.pallas_call(functools.partial(kern, MODE), out_shape=[jax.ShapeDtypeSt...]
    ppermute x14 -> x0, waiting for transfers between devices: 25 us -> none  [the longest x10 15.9 us: turned(): lax.ppermute(value, axes[0], [(i, (i + step[0]) % count) for i in range(c...]
    ppermute x14 -> x0, starting transfers between devices: 20.6 us -> none  [the longest x10 18.3 us: turned(): lax.ppermute(value, axes[0], [(i, (i + step[0]) % count) for i in range(c...]
    unnamed x28, local copies, waits for them, and re-layouts: 5.56 us -> 9.43 us
    slice x8 -> x0, local copies, waits for them, and re-layouts: 2.17 us -> none  [the longest x1 0.99 us: local(): bx = turned(hs[192:320], ('slab',), (1,))]
  transfers between devices with their start and end apart: 14 -> 0, of which waited for: 9 -> 0; matrix products, arithmetic and copies ran while one was open for 1% -> 0% of each run, Pallas kernels for 0% -> 0%
where the time goes in v2:
time: 167 us; the launch traced here: 166 us
  Pallas kernels  155 us (93%)
  local copies, waits for them, and re-layouts  10.2 us (6%)
    pallas_call x1, Pallas kernels, compute(): pl.pallas_call(functools.partial(kern, MODE), out_shape=[jax.ShapeDtypeSt...  114 us
    pallas_call x1, Pallas kernels, relayout(): pl.pallas_call(relayout_kernel, out_shape=[jax.ShapeDtypeStruct((r, 512),...  27.2 us
    pallas_call x1, Pallas kernels, combine(): pl.pallas_call(combine_kernel, out_shape=[jax.ShapeDtypeStruct((256, 128)...  13.6 us
    unnamed x28, local copies, waits for them, and re-layouts  9.43 us

profile of v2, /device:TPU:1, one launch (start us, length us, event | category | flops | bytes accessed | tf_op | source)
XLA Modules:
  0.0 166.2 jit_solution(12640545165802946435)
XLA Ops:
  0.6 0.0 copy-start.12
  0.6 0.6 pad_maximum_fusion.sc_ref
  1.2 0.1 copy-done.12
  1.3 0.1 reshape_reshape.4.cnt_ref
  1.4 0.0 copy-start.11
  1.4 0.6 reshape.16.cnt_ref
  2.0 0.0 copy-done.11
  2.1 0.0 copy-start.2
  2.1 1.0 copy-done.2
  3.1 27.2 %relayout.1 = (f32[256,512]{1,0:T(8,128)S(1)}, f32[128,512]{1,0:T(8,128)S(1)}, f32[64,512]{1,0:T(8,128)S(1)}, f32[128,512]{1,0:T(8,128)S(1)}, f32[64,512]{1,0:T(8,128)S(1)}, /*index=5*/f32[64,512]{1,0:T(8,128)S(1)}) custom-call(f32[256,4,128]{2,1,0:T(4,128)S(1)} %bitcast.5, s32[1,256]{1,0:T(1,128)S(1)} %copy-done.11, s32[1,256]{1,0:T(1,128)S(1)} %reshape_reshape.4.cnt_ref), custom_call_target="tpu_custom_call" | custom-call | tf_op jit(solution)/shard_map/relayout/pallas_call | solution.py:341
  30.4 0.0 copy-start
  30.4 0.8 copy-done
  31.1 0.0 copy-start.4
  31.1 0.7 copy-done.4
  31.9 0.0 copy-start.5
  31.9 0.7 copy-done.5
  32.5 0.0 copy-start.6
  32.5 0.7 copy-done.6
  33.2 0.0 copy-start.7
  33.2 0.7 copy-done.7
  33.9 0.6 copy-done.8
  34.5 0.0 copy-start.1
  34.5 113.9 %pairs.1 = (f32[256,128]{1,0:T(8,128)}, f32[256,128]{1,0:T(8,128)}, f32[448,256]{1,0:T(8,128)}) custom-call(f32[2]{0:T(128)} %pad_maximum_fusion.sc_ref, s32[256]{0:T(256)} %reshape.16.cnt_ref, f32[256,512]{1,0:T(8,128)} %copy-done, f32[128,512]{1,0:T(8,128)} %copy-done.4, f32[64,512]{1,0:T(8,128)} %copy-done.6, f32[128,512]{1,0:T(8,128)} %copy-done.5, ...), custom_call_target="tpu_custom_call" | custom-call | tf_op jit(solution)/shard_map/pairs/pallas_call | solution.py:235
  148.4 0.0 copy-done.1
  148.4 0.0 copy-start.3
  148.5 1.0 copy-done.3
  149.5 0.0 copy-start.9
  149.5 0.9 copy-done.9
  150.4 0.9 copy-done.10
  151.3 13.6 %combine.1 = (f32[256,128]{1,0:T(8,128)S(1)}, f32[256,128]{1,0:T(8,128)S(1)}) custom-call(f32[256,128]{1,0:T(8,128)S(1)} %copy-done.9, f32[256,128]{1,0:T(8,128)S(1)} %copy-done.10, f32[448,256]{1,0:T(8,128)S(1)} %copy-done.3, f32[256,512]{1,0:T(8,128)S(1)} %copy-done.1, s32[1,256]{1,0:T(1,128)S(1)} %reshape_reshape.4.cnt_ref), custom_call_target="tpu_custom_call" | custom-call | tf_op jit(solution)/shard_map/combine/pallas_call | solution.py:383
  164.9 0.7 copy.7
  165.5 0.7 copy.8
  (2 shorter events, 0.0 us)
Async XLA Ops:
  0.6 0.7 copy-start.12
  1.4 0.7 copy-start.11
  2.1 1.0 copy-start.2
  30.4 0.8 copy-start
  31.1 0.7 copy-start.4
  31.9 0.7 copy-start.5
  32.5 0.7 copy-start.6
  33.2 0.7 copy-start.7
  33.9 0.7 copy-start.8
  34.5 113.9 %copy-start.1 = (f32[256,512]{1,0:T(8,128)S(1)}, f32[256,512]{1,0:T(8,128)}, u32[]{:S(2)}) copy-start(f32[256,512]{1,0:T(8,128)} %copy-done) | copy-start | bytes 1572868
  148.4 1.0 copy-start.3
  149.5 0.9 copy-start.9
  150.4 0.9 copy-start.10

commit v3 on v2

v3 whole, which is shorter than its diff:
```python
import functools
import jax, jax.numpy as jnp
from jax import lax
from jax.experimental import pallas as pl
from jax.experimental.pallas import tpu as pltpu
from jax.sharding import PartitionSpec as P

f32, bf16 = jnp.float32, jnp.bfloat16
SENT = 100.0
ZP = 66
ref_density = 268.0825731
N_SLAB, N_DOM = 4, 32

OFFS = [(0, 0, 0), (0, 0, 1)] + [(dx, dy, dz) for dx, dy in ((0, 1), (1, -1), (1, 0), (1, 1)) for dz in (-1, 0, 1)]
NT = len(OFFS)
FR = 5


def split3(v):
    h = v.astype(bf16).astype(f32)
    r = v - h
    m = r.astype(bf16).astype(f32)
    return h, m, r - m


def split2(v):
    h = v.astype(bf16).astype(f32)
    m = (v - h).astype(bf16).astype(f32)
    return h, m, h + m


def left(h, m):
    return [-2.0 * h, -2.0 * h, -2.0 * m, -2.0 * m]


def right(h, m):
    return [h, m, h, m]


def build_cols(p_ref, row0, col, x0, y0, own_cell, b_ref, f_ref, a_ref, stage, stage_a):
    @pl.loop(0, 8)
    def _(k):
        z0 = k * 8
        rows = pl.ds(pl.multiple_of(row0 + z0, 8), 8)
        zc = (lax.broadcasted_iota(jnp.int32, (8, 128), 0) + z0).astype(f32) + 0.5
        xh, xm, x = split2(p_ref[rows, 0:128] - x0)
        yh, ym, y = split2(p_ref[rows, 128:256] - y0)
        zh, zm, z = split2(p_ref[rows, 256:384] - zc)
        f = p_ref[rows, 384:512]
        f_ref[pl.ds(col * ZP + 1 + z0, 8), :] = f
        xy = x * x + y * y
        terms = dict(enumerate(right(xh, xm) + right(yh, ym) + list(split3(xy + z * z))))
        terms.update(enumerate(right(zh, zm), 16))
        for r, v in terms.items():
            stage[pl.ds(r, 8, stride=32), :] = v
        b_ref[pl.ds(pl.multiple_of((col * ZP + 1 + z0) * 32, 32), 256), :] = stage[...].astype(bf16)
        if own_cell is None:
            return
        terms = dict(enumerate(left(xh, xm) + left(yh, ym)))
        for k2, s in enumerate((-1.0, 0.0, 1.0)):
            h, m, zs = split2(z - s)
            terms.update(enumerate(left(h, m) + list(split3(xy + zs * zs)), 16 + 16 * k2))
        terms.update(enumerate(split3(f), 23))
        for r, v in terms.items():
            stage_a[pl.ds(r, 8, stride=64), :] = v
        for j in range(8):
            t = stage_a[j * 64:j * 64 + 64, :].T
            a_ref[pl.ds(pl.multiple_of((own_cell + z0 + j) * 128, 128), 128), :] = t.astype(bf16)


def cell_of(cell):
    cx, cy, z = cell // 128, (cell // 64) % 2, cell % 64
    return [((cx + dx) * 4 + cy + 1 + dy) * ZP + 1 + z + dz for dx, dy, dz in OFFS]


def make_d(cell, d_ref, a_ref, b_ref):
    a = a_ref[pl.ds(pl.multiple_of(cell * 128, 128), 128), :]
    zero = jnp.zeros((16, 128), bf16)
    ri = lax.broadcasted_iota(jnp.int32, (16, 128), 0)
    pick = jnp.where((ri >= 7) & (ri < 10), 1.0, 0.0).astype(bf16)
    ws = []
    for (dx, dy, dz), c in zip(OFFS, cell_of(cell)):
        b = b_ref[pl.ds(pl.multiple_of(c * 32, 32), 32), :]
        ws.append(jnp.concatenate([b[:16]] + [b[16:] if k == dz else zero for k in (-1, 0, 1)], 0))
    ws.append(jnp.concatenate([zero, pick, zero, zero], 0))

    def part(t, r):
        w = jnp.concatenate(ws[t:t + 2], 1)
        d_ref[r:r + 32, 128 * t:128 * t + w.shape[1]] = jnp.dot(a[r:r + 32], w, preferred_element_type=f32)
    return [functools.partial(part, t, r) for t in range(0, NT + 1, 2) for r in range(0, 128, 32)]


def finish(cell, an_ref, as_ref, out_ref):
    out_ref[0, pl.ds(cell, 1), :] = jnp.sum(an_ref[...].T, axis=0, keepdims=True)
    out_ref[1, pl.ds(cell, 1), :] = jnp.sum(as_ref[...].T, axis=0, keepdims=True)


def pair_sums(R, cell, d_ref, an_ref, as_ref, f_ref, jn_ref, js_ref, parts):
    if R == 0:
        for part in parts:
            part()
        return
    cs = cell_of(cell)
    fj = [jnp.broadcast_to(f_ref[pl.ds(c, 1), :], (8, 128)) for c in cs]
    f0 = fj[0]
    for v in fj[1:]:
        f0 = f0 + v
    cn = [jnp.full((8, 128), -(R // 8.0), f32) for _ in cs]
    fi0 = d_ref[0:8, 128 * NT:128 * NT + 128]
    for r in range(8, R, 8):
        fi0 = fi0 + d_ref[r:r + 8, 128 * NT:128 * NT + 128]
    cm = [-fi0 for _ in cs]
    for r in range(0, R, 8):
        fi = d_ref[r:r + 8, 128 * NT:128 * NT + 128]
        an = jnp.full((8, 128), -float(NT), f32)
        am = -f0
        for t in range(NT):
            d = d_ref[r:r + 8, 128 * t:128 * t + 128]
            q = jnp.maximum(lax.rsqrt(jnp.maximum(d, 0.01)), 1.0)
            an = an + q
            am = am + q * fj[t]
            if t:
                cn[t] = cn[t] + q
                cm[t] = cm[t] + q * fi
        an_ref[r:r + 8, :] = an
        as_ref[r:r + 8, :] = am
        for part in parts[min(FR * r * len(parts) // R // 4, len(parts)):min(FR * (r + 8) * len(parts) // R // 4, len(parts))]:
            part()
    rows = [pl.ds(pl.multiple_of(c * 8, 8), 8) for c in cs]
    olds = [(jn_ref[rows[t], :], js_ref[rows[t], :]) for t in range(1, NT)]
    for t in range(1, NT):
        jn_ref[rows[t], :] = olds[t - 1][0] + cn[t]
        js_ref[rows[t], :] = olds[t - 1][1] + cm[t]


def tree(v, lo, hi, run):
    if hi - lo == 1:
        run(lo)
        return
    mid = (lo + hi) // 2

    @pl.when(v < mid)
    def _():
        tree(v, lo, mid, run)

    @pl.when(v >= mid)
    def _():
        tree(v, mid, hi, run)


def kern(MODE, sc_ref, cnt_ref, cells, out_ref,
         a_ref, b_ref, f_ref, jn_ref, js_ref, stage, stage_a, d0, d1, an0, as0, an1, as1):
    x0 = sc_ref[0]
    y0 = sc_ref[1]
    ra = lax.broadcasted_iota(jnp.int32, stage_a.shape, 0) % 64
    stage_a[...] = jnp.where((ra >= 8) & (ra < 11), 1.0, 0.0)
    rb = lax.broadcasted_iota(jnp.int32, stage.shape, 0) % 32
    stage[...] = jnp.where((rb >= 20) & (rb < 23), 1.0, 0.0)
    ri = lax.broadcasted_iota(jnp.int32, (32, 128), 0)
    rim = (jnp.where(ri == 8, SENT * SENT, 0.0) + jnp.where((ri >= 20) & (ri < 23), 1.0, 0.0)).astype(bf16)

    @pl.loop(0, 12)
    def _(col):
        for zz in (0, ZP - 1):
            b_ref[pl.ds(pl.multiple_of((col * ZP + zz) * 32, 32), 32), :] = rim
            f_ref[pl.ds(col * ZP + zz, 1), :] = jnp.zeros((1, 128), f32)

    @pl.loop(0, 12)
    def _(k):
        rows = pl.ds(pl.multiple_of(k * 8 * ZP, 8), 8 * ZP)
        jn_ref[rows, :] = jnp.zeros((8 * ZP, 128), f32)
        js_ref[rows, :] = jnp.zeros((8 * ZP, 128), f32)

    b = functools.partial(build_cols, x0=x0, y0=y0, b_ref=b_ref, f_ref=f_ref, a_ref=a_ref, stage=stage, stage_a=stage_a)

    @pl.loop(0, 4)
    def _(k):
        b(cells, k * 64, (k // 2) * 4 + k % 2 + 1, own_cell=k * 64)

    @pl.loop(0, 7)
    def _(k):
        col = jnp.where(k < 2, 3 + 4 * k, jnp.where(k < 3, 4, jnp.where(k < 6, 6 + k, 8)))
        b(cells, 256 + k * 64, col, own_cell=None)

    if MODE == "build":
        out_ref[...] = jnp.zeros_like(out_ref)
        return
    for part in make_d(0, d0, a_ref, b_ref):
        part()
    bufs = ((d0, an0, as0), (d1, an1, as1))

    @pl.loop(0, 128)
    def _(i):
        for p in range(2):
            cell = i * 2 + p
            nxt = jnp.minimum(cell + 1, 255)
            prev = jnp.maximum(cell - 1, 0)
            d, an, am = bufs[p]
            dn, anp, amp = bufs[1 - p]

            def run(k):
                parts = make_d(nxt, dn, a_ref, b_ref)
                finish(prev, anp, amp, out_ref)
                pair_sums(16 * k, cell, d, an, am, f_ref, jn_ref, js_ref, parts)
            tree((cnt_ref[cell] + 15) // 16, 0, 9, run)
    finish(255, an1, as1, out_ref)

    def side(col, z0, ref):
        base = (col * ZP + 1 + z0) * 8
        v = ref[pl.ds(base, 8, stride=8), :]
        for k in range(1, 8):
            v = v + ref[pl.ds(base + k, 8, stride=8), :]
        return v

    @pl.loop(0, 32)
    def _(k):
        cx, cy, z0 = k // 16, (k // 8) % 2, (k % 8) * 8
        rows = pl.ds(pl.multiple_of(k * 8, 8), 8)
        out_ref[0, rows, :] += side(cx * 4 + cy + 1, z0, jn_ref)
        out_ref[1, rows, :] += side(cx * 4 + cy + 1, z0, js_ref)

    @pl.loop(0, 8)
    def _(k):
        for h, col in enumerate((3, 7, 4, 9, 10, 11, 8)):
            rows = pl.ds(pl.multiple_of(256 + h * 64 + k * 8, 8), 8)
            out_ref[0, rows, :] = side(col, k * 8, jn_ref)
            out_ref[1, rows, :] = side(col, k * 8, js_ref)


def compute(sc, cnt, cells, MODE="full"):
    vm = pl.BlockSpec(memory_space=pltpu.VMEM)
    sm = pl.BlockSpec(memory_space=pltpu.SMEM)
    return pl.pallas_call(
        functools.partial(kern, MODE),
        out_shape=jax.ShapeDtypeStruct((2, 704, 128), f32),
        in_specs=[sm, sm, vm], out_specs=vm,
        scratch_shapes=[pltpu.VMEM((256 * 128, 64), bf16), pltpu.VMEM((12 * ZP * 32, 128), bf16),
                        pltpu.VMEM((12 * ZP, 128), f32), pltpu.VMEM((12 * ZP * 8, 128), f32), pltpu.VMEM((12 * ZP * 8, 128), f32),
                        pltpu.VMEM((256, 128), f32), pltpu.VMEM((512, 128), f32)]
        + [pltpu.VMEM((128, 128 * (NT + 1)), f32)] * 2 + [pltpu.VMEM((128, 128), f32)] * 4,
        compiler_params=pltpu.CompilerParams(vmem_limit_bytes=56 * 2**20),
        name="pairs",
    )(sc, cnt, cells)


def far(ds, dd):
    slab = lax.rem(lax.axis_index("slab") + (ds + N_SLAB), N_SLAB)
    dom = lax.rem(lax.axis_index("dom") + (dd + N_DOM), N_DOM)
    return (slab, dom)


def copy_to(src, dst, send, recv, where):
    return pltpu.make_async_remote_copy(
        src_ref=src, dst_ref=dst, send_sem=send, recv_sem=recv, device_id=far(*where),
        device_id_type=pl.DeviceIdType.MESH)


def greet(senders):
    barrier = pltpu.get_barrier_semaphore()
    for where in senders:
        pl.semaphore_signal(barrier, inc=1, device_id=far(*where), device_id_type=pl.DeviceIdType.MESH)
    pl.semaphore_wait(barrier, len(senders))


def picked(onehot, v, dims):
    out = None
    for part in reversed(split3(v)):
        p = lax.dot_general(onehot, part.astype(bf16), (dims, ((), ())), preferred_element_type=f32)
        out = p if out is None else out + p
    return out


def iota(shape, dim):
    return lax.broadcasted_iota(jnp.int32, shape, dim).astype(f32)


FAR = (0, 4, 1, 3)
HALO = ((0, 64, (-1, -1), 576), (64, 64, (-1, 1), 640), (0, 128, (-1, 0), 448), (0, 64, (0, -1), 256),
        (128, 64, (0, -1), 320), (192, 64, (0, 1), 384))


def relayout_kernel(x_ref, dest_ref, cnt_ref, cells, sent, got, parts, s1, r1, s2, r2):
    me = lax.axis_index("dom")
    greet([(0, -2), (0, -1), (0, 1), (0, 2), (1, 0), (1, 1), (1, -1)])
    dest = dest_ref[...]
    dom = lax.shift_right_logical(dest, 8)
    shift = (dom - me).astype(f32)
    shift = jnp.where(shift < -16.0, shift + 32.0, jnp.where(shift > 16.0, shift - 32.0, shift)) + 2.0
    local = (dest - dom * 256).astype(f32)
    chosen = jnp.where(iota((8, 256), 0) == shift, 1.0, 0.0)
    lower = jnp.where(iota((256, 256), 0) <= iota((256, 256), 1), 1.0, 0.0).astype(bf16)
    rank = jnp.dot(chosen.astype(bf16), lower, preferred_element_type=f32)
    rank = jnp.sum(chosen * rank, axis=0, keepdims=True) - 1.0
    slot = shift * 64.0 + rank
    xs = [x_ref[:, c, :] for c in range(4)]
    diag = jnp.where(iota((256, 256), 0) == iota((256, 256), 1), 1.0, 0.0)
    tag = jnp.broadcast_to(jnp.sum(diag * local, axis=1, keepdims=True) + 1.0, (256, 128))
    for c in range(4):
        for p, v in enumerate(split3(xs[c])):
            parts[p, :, 128 * c:128 * c + 128] = v.astype(bf16)
    tag = tag.astype(bf16)

    def send_part(k, dst):
        pack = jnp.where(iota((64, 256), 0) + 64.0 * k == slot, 1.0, 0.0).astype(bf16)
        out = [jnp.dot(pack, parts[p], preferred_element_type=f32) for p in (2, 1, 0)]
        dst[k, :, 0:512] = out[0] + out[1] + out[2]
        dst[k, :, 512:640] = jnp.dot(pack, tag, preferred_element_type=f32)
    first = []
    for k in FAR:
        send_part(k, sent)
        c = copy_to(sent.at[k], got.at[k], s1.at[k], r1.at[k], (0, k - 2))
        c.start()
        first.append(c)
    send_part(2, got)
    count = jnp.sum(diag * cnt_ref[...].astype(f32), axis=1, keepdims=True)
    filled = iota((256, 128), 1) < count
    for c in first:
        c.wait_recv()
    places = []
    for k in range(5):
        label = got[k, :, 512:640]
        lanes = iota((64, 128), 1)
        places.append(jnp.concatenate(
            [jnp.where(label == lanes + 1.0, 1.0, 0.0), jnp.where(label == lanes + 129.0, 1.0, 0.0)], 1))
    place = jnp.concatenate(places, 0).T.astype(bf16)
    total = picked(place, jnp.concatenate([got[k, :, 0:512] for k in range(5)], 0), ((1,), (0,)))
    x0 = (lax.axis_index("slab") * 2 + 1).astype(f32)
    cells[0:256, 0:128] = jnp.where(filled, total[:, 0:128], x0 + SENT)
    cells[0:256, 128:384] = total[:, 128:384]
    cells[0:256, 384:512] = jnp.where(filled, total[:, 384:512], 0.0)
    second = []
    for k, (row, rows, where, there) in enumerate(HALO):
        c = copy_to(cells.at[pl.ds(row, rows)], cells.at[pl.ds(there, rows)], s2.at[k], r2.at[k], where)
        c.start()
        second.append(c)
    for c in first:
        c.wait_send()
    for c in second:
        c.wait()


def relayout(x, dest, count):
    vm = pl.BlockSpec(memory_space=pltpu.VMEM)
    return pl.pallas_call(
        relayout_kernel,
        out_shape=jax.ShapeDtypeStruct((704, 512), f32),
        in_specs=[vm] * 3, out_specs=vm,
        scratch_shapes=[pltpu.VMEM((5, 64, 640), f32)] * 2 + [pltpu.VMEM((3, 256, 512), bf16)]
        + [pltpu.SemaphoreType.DMA((5,))] * 2 + [pltpu.SemaphoreType.DMA((6,))] * 2,
        compiler_params=pltpu.CompilerParams(collective_id=0, has_side_effects=True, vmem_limit_bytes=32 * 2**20),
        name="relayout",
    )(x, dest, count)


BACK = ((320, 64, (1, 1)), (384, 64, (1, -1)), (192, 128, (1, 0)), (0, 128, (0, 1)), (128, 64, (0, -1)))


def combine_kernel(sums, cells, cnt_ref, dens, lap, got, field, s1, r1, fsem):
    greet([(0, -1), (0, 1), (-1, 0), (-1, -1), (-1, 1)])
    fetch = pltpu.make_async_copy(cells.at[pl.ds(0, 256), pl.ds(384, 128)], field, fsem)
    fetch.start()
    copies = []
    for k, (row, rows, where) in enumerate(BACK):
        c = copy_to(sums.at[:, pl.ds(256 + row, rows)], got.at[:, pl.ds(row, rows)], s1.at[k], r1.at[k], where)
        c.start()
        copies.append(c)
    diag = jnp.where(iota((256, 256), 0) == iota((256, 256), 1), 1.0, 0.0)
    count = jnp.sum(diag * cnt_ref[...].astype(f32), axis=1, keepdims=True)
    fetch.wait()
    for c in copies:
        c.wait()
    own = lax.rsqrt(jnp.full((64, 128), 0.01, f32)) - 1.0
    lists = ((0, 192, 320), (256, 384), (64,), (128,))
    for q in range(4):
        rows = slice(64 * q, 64 * q + 64)
        n = sums[0, rows, :]
        s = sums[1, rows, :]
        for r in lists[q]:
            n = n + got[0, r:r + 64, :]
            s = s + got[1, r:r + 64, :]
        filled = iota((64, 128), 1) < count[rows]
        dens[rows, :] = jnp.where(filled, (n - own) / ref_density, 0.0)
        lap[rows, :] = jnp.where(filled, (s - field[rows, :] * n) / ref_density, 0.0)


def combine(sums, cells, count):
    vm = pl.BlockSpec(memory_space=pltpu.VMEM)
    return pl.pallas_call(
        combine_kernel,
        out_shape=[jax.ShapeDtypeStruct((256, 128), f32)] * 2,
        in_specs=[vm, pl.BlockSpec(memory_space=pl.ANY), vm], out_specs=[vm] * 2,
        scratch_shapes=[pltpu.VMEM((2, 448, 128), f32), pltpu.VMEM((256, 128), f32), pltpu.SemaphoreType.DMA((5,)), pltpu.SemaphoreType.DMA((5,)),
                        pltpu.SemaphoreType.DMA],
        compiler_params=pltpu.CompilerParams(collective_id=1, has_side_effects=True, vmem_limit_bytes=16 * 2**20),
        name="combine",
    )(sums, cells, count)


def local(incoming, dest, counts):
    count = counts.reshape(256)
    x0 = (lax.axis_index("slab") * 2 + 1).astype(f32)
    y0 = (lax.axis_index("dom") * 2 + 1).astype(f32)
    cells = relayout(incoming.reshape(256, 4, 128), dest, count.reshape(1, 256))
    sums = compute(jnp.stack([x0, y0]), count, cells)
    density, laplace = combine(sums, cells, count.reshape(1, 256))
    return density.reshape(2, 2, 64, 128), laplace.reshape(2, 2, 64, 128)


def solution(mesh):
    in_specs = (P("slab", "dom", None, None), P("slab", "dom"), P("slab", "dom", None))
    out_specs = (P("slab", "dom", None, None), P("slab", "dom", None, None))
    return jax.shard_map(local, mesh=mesh, in_specs=in_specs, out_specs=out_specs, check_vma=False)
```

time: 167 us -> 156 us (0.934)
  Pallas kernels: 155 us -> 145 us
    pallas_call x2, Pallas kernels: 141 us -> 133 us  [the longest x1 106 us: compute(): pl.pallas_call(functools.partial(kern, MODE), out_shape=jax.ShapeDtypeStr...]
    unnamed x28 -> x12, local copies, waits for them, and re-layouts: 9.43 us -> 6.62 us
where the time goes in v3:
time: 156 us; the launch traced here: 155 us
  Pallas kernels  145 us (93%)
  local copies, waits for them, and re-layouts  8.7 us (6%)
    pallas_call x1, Pallas kernels, compute(): pl.pallas_call(functools.partial(kern, MODE), out_shape=jax.ShapeDtypeStr...  106 us
    pallas_call x1, Pallas kernels, relayout(): pl.pallas_call(relayout_kernel, out_shape=jax.ShapeDtypeStruct((704, 512)...  27 us
    pallas_call x1, Pallas kernels, combine(): pl.pallas_call(combine_kernel, out_shape=[jax.ShapeDtypeStruct((256, 128)...  12.1 us
    unnamed x12, local copies, waits for them, and re-layouts  6.62 us

profile of v3, /device:TPU:1, one launch (start us, length us, event | category | flops | bytes accessed | tf_op | source)
XLA Modules:
  0.0 155.0 jit_solution(12015799028946119519)
XLA Ops:
  0.6 0.6 pad_maximum_fusion.sc_ref
  1.3 0.8 reshape_reshape.4.cnt_ref
  2.0 1.3 reshape.16.cnt_ref
  3.4 0.0 copy-start.3
  3.4 1.0 copy-done.3
  4.4 0.0 copy-start.4
  4.4 0.7 copy-done.4
  5.1 27.0 %relayout.1.cells = f32[704,512]{1,0:T(8,128)S(1)} custom-call(f32[256,4,128]{2,1,0:T(4,128)S(1)} %bitcast.5, s32[1,256]{1,0:T(1,128)S(1)} %copy-done.4, s32[1,256]{1,0:T(1,128)S(1)} %reshape_reshape.4.cnt_ref), custom_call_target="tpu_custom_call" | custom-call | tf_op jit(solution)/shard_map/relayout/pallas_call | solution.py:344
  32.1 0.0 copy-start
  32.1 1.1 copy-done
  33.2 105.9 %pairs.1.sums = f32[2,704,128]{2,1,0:T(8,128)} custom-call(f32[2]{0:T(128)} %pad_maximum_fusion.sc_ref, s32[256]{0:T(256)} %reshape.16.cnt_ref, f32[704,512]{1,0:T(8,128)} %copy-done), custom_call_target="tpu_custom_call" | custom-call | tf_op jit(solution)/shard_map/pairs/pallas_call | solution.py:233
  139.1 0.0 copy-start.1
  139.1 1.4 copy-done.1
  140.5 0.0 copy-start.2
  140.5 1.1 copy-done.2
  141.6 12.1 %combine.1 = (f32[256,128]{1,0:T(8,128)S(1)}, f32[256,128]{1,0:T(8,128)S(1)}) custom-call(f32[2,704,128]{2,1,0:T(8,128)S(1)} %copy-done.2, f32[704,512]{1,0:T(8,128)S(1)} %copy-done.1, s32[1,256]{1,0:T(1,128)S(1)} %reshape_reshape.4.cnt_ref), custom_call_target="tpu_custom_call" | custom-call | tf_op jit(solution)/shard_map/combine/pallas_call | solution.py:388
  153.7 0.7 copy.7
  154.4 0.7 copy.8
Async XLA Ops:
  3.4 1.0 copy-start.3
  4.4 0.7 copy-start.4
  32.1 1.1 copy-start
  139.1 1.4 copy-start.1
  140.5 1.1 copy-start.2

commit v4 on v3

--- a/solution.py
+++ b/solution.py
@@ -148,10 +148,13 @@
         tree(v, mid, hi, run)
 
 
-def kern(MODE, sc_ref, cnt_ref, cells, out_ref,
+def centre():
+    return (lax.axis_index("slab") * 2 + 1).astype(f32), (lax.axis_index("dom") * 2 + 1).astype(f32)
+
+
+def kern(cnt_ref, cells, out_ref,
          a_ref, b_ref, f_ref, jn_ref, js_ref, stage, stage_a, d0, d1, an0, as0, an1, as1):
-    x0 = sc_ref[0]
-    y0 = sc_ref[1]
+    x0, y0 = centre()
     ra = lax.broadcasted_iota(jnp.int32, stage_a.shape, 0) % 64
     stage_a[...] = jnp.where((ra >= 8) & (ra < 11), 1.0, 0.0)
     rb = lax.broadcasted_iota(jnp.int32, stage.shape, 0) % 32
@@ -182,9 +185,6 @@
         col = jnp.where(k < 2, 3 + 4 * k, jnp.where(k < 3, 4, jnp.where(k < 6, 6 + k, 8)))
         b(cells, 256 + k * 64, col, own_cell=None)
 
-    if MODE == "build":
-        out_ref[...] = jnp.zeros_like(out_ref)
-        return
     for part in make_d(0, d0, a_ref, b_ref):
         part()
     bufs = ((d0, an0, as0), (d1, an1, as1))
@@ -202,7 +202,7 @@
                 parts = make_d(nxt, dn, a_ref, b_ref)
                 finish(prev, anp, amp, out_ref)
                 pair_sums(16 * k, cell, d, an, am, f_ref, jn_ref, js_ref, parts)
-            tree((cnt_ref[cell] + 15) // 16, 0, 9, run)
+            tree((cnt_ref[cell // 128, (cell // 64) % 2, cell % 64] + 15) // 16, 0, 9, run)
     finish(255, an1, as1, out_ref)
 
     def side(col, z0, ref):
@@ -227,20 +227,20 @@
             out_ref[1, rows, :] = side(col, k * 8, js_ref)
 
 
-def compute(sc, cnt, cells, MODE="full"):
+def compute(cnt, cells):
     vm = pl.BlockSpec(memory_space=pltpu.VMEM)
     sm = pl.BlockSpec(memory_space=pltpu.SMEM)
     return pl.pallas_call(
-        functools.partial(kern, MODE),
+        kern,
         out_shape=jax.ShapeDtypeStruct((2, 704, 128), f32),
-        in_specs=[sm, sm, vm], out_specs=vm,
+        in_specs=[sm, vm], out_specs=vm,
         scratch_shapes=[pltpu.VMEM((256 * 128, 64), bf16), pltpu.VMEM((12 * ZP * 32, 128), bf16),
                         pltpu.VMEM((12 * ZP, 128), f32), pltpu.VMEM((12 * ZP * 8, 128), f32), pltpu.VMEM((12 * ZP * 8, 128), f32),
                         pltpu.VMEM((256, 128), f32), pltpu.VMEM((512, 128), f32)]
         + [pltpu.VMEM((128, 128 * (NT + 1)), f32)] * 2 + [pltpu.VMEM((128, 128), f32)] * 4,
-        compiler_params=pltpu.CompilerParams(vmem_limit_bytes=56 * 2**20),
+        compiler_params=pltpu.CompilerParams(vmem_limit_bytes=30 * 2**20),
         name="pairs",
-    )(sc, cnt, cells)
+    )(cnt, cells)
 
 
 def far(ds, dd):
@@ -275,13 +275,15 @@
 
 
 FAR = (0, 4, 1, 3)
-HALO = ((0, 64, (-1, -1), 576), (64, 64, (-1, 1), 640), (0, 128, (-1, 0), 448), (0, 64, (0, -1), 256),
-        (128, 64, (0, -1), 320), (192, 64, (0, 1), 384))
-
-
-def relayout_kernel(x_ref, dest_ref, cnt_ref, cells, sent, got, parts, s1, r1, s2, r2):
+HALO = ((0, 64, (-1, 0), 448), (64, 64, (-1, 0), 512), (0, 64, (0, -1), 256), (128, 64, (0, -1), 320),
+        (192, 64, (0, 1), 384), (448, 64, (0, -1), 576), (512, 64, (0, 1), 640))
+
+
+def relayout_kernel(x_any, dest_ref, cnt_ref, cells, x_ref, sent, got, parts, s1, r1, s2, r2, xsem):
+    fetch = pltpu.make_async_copy(x_any, x_ref, xsem)
+    fetch.start()
     me = lax.axis_index("dom")
-    greet([(0, -2), (0, -1), (0, 1), (0, 2), (1, 0), (1, 1), (1, -1)])
+    greet([(0, -2), (0, -1), (0, 1), (0, 2), (1, 0)])
     dest = dest_ref[...]
     dom = lax.shift_right_logical(dest, 8)
     shift = (dom - me).astype(f32)
@@ -292,19 +294,18 @@
     rank = jnp.dot(chosen.astype(bf16), lower, preferred_element_type=f32)
     rank = jnp.sum(chosen * rank, axis=0, keepdims=True) - 1.0
     slot = shift * 64.0 + rank
-    xs = [x_ref[:, c, :] for c in range(4)]
-    diag = jnp.where(iota((256, 256), 0) == iota((256, 256), 1), 1.0, 0.0)
-    tag = jnp.broadcast_to(jnp.sum(diag * local, axis=1, keepdims=True) + 1.0, (256, 128))
+    tag = jnp.broadcast_to(local + 1.0, (8, 256)).astype(bf16)
+    fetch.wait()
     for c in range(4):
-        for p, v in enumerate(split3(xs[c])):
+        for p, v in enumerate(split3(x_ref[pl.ds(c, 256, stride=4), :])):
             parts[p, :, 128 * c:128 * c + 128] = v.astype(bf16)
-    tag = tag.astype(bf16)
 
     def send_part(k, dst):
         pack = jnp.where(iota((64, 256), 0) + 64.0 * k == slot, 1.0, 0.0).astype(bf16)
         out = [jnp.dot(pack, parts[p], preferred_element_type=f32) for p in (2, 1, 0)]
-        dst[k, :, 0:512] = out[0] + out[1] + out[2]
-        dst[k, :, 512:640] = jnp.dot(pack, tag, preferred_element_type=f32)
+        dst[k, 0:64, :] = out[0] + out[1] + out[2]
+        dst[k, 64:72, 0:64] = lax.dot_general(tag, pack, (((1,), (1,)), ((), ())), preferred_element_type=f32)
+    sent[:, 64:72, :] = jnp.zeros((5, 8, 512), f32)
     first = []
     for k in FAR:
         send_part(k, sent)
@@ -312,31 +313,32 @@
         c.start()
         first.append(c)
     send_part(2, got)
-    count = jnp.sum(diag * cnt_ref[...].astype(f32), axis=1, keepdims=True)
+    diag = jnp.where(iota((256, 256), 0) == iota((256, 256), 1), 1.0, 0.0)
+    count = jnp.concatenate([cnt_ref[a, b:b + 1, :] for a in range(2) for b in range(2)], 1).astype(f32)
+    count = jnp.sum(diag * count, axis=1, keepdims=True)
     filled = iota((256, 128), 1) < count
     for c in first:
         c.wait_recv()
-    places = []
-    for k in range(5):
-        label = got[k, :, 512:640]
-        lanes = iota((64, 128), 1)
-        places.append(jnp.concatenate(
-            [jnp.where(label == lanes + 1.0, 1.0, 0.0), jnp.where(label == lanes + 129.0, 1.0, 0.0)], 1))
-    place = jnp.concatenate(places, 0).T.astype(bf16)
-    total = picked(place, jnp.concatenate([got[k, :, 0:512] for k in range(5)], 0), ((1,), (0,)))
-    x0 = (lax.axis_index("slab") * 2 + 1).astype(f32)
+    label = jnp.concatenate([got[k, 64:65, 0:64] for k in range(5)], 1)
+    place = jnp.where(iota((256, 320), 0) + 1.0 == label, 1.0, 0.0).astype(bf16)
+    total = picked(place, jnp.concatenate([got[k, 0:64, :] for k in range(5)], 0), ((1,), (0,)))
+    x0, _ = centre()
     cells[0:256, 0:128] = jnp.where(filled, total[:, 0:128], x0 + SENT)
     cells[0:256, 128:384] = total[:, 128:384]
     cells[0:256, 384:512] = jnp.where(filled, total[:, 384:512], 0.0)
     second = []
     for k, (row, rows, where, there) in enumerate(HALO):
+        if k >= 5:
+            second[k - 5].wait_recv()
         c = copy_to(cells.at[pl.ds(row, rows)], cells.at[pl.ds(there, rows)], s2.at[k], r2.at[k], where)
         c.start()
         second.append(c)
     for c in first:
         c.wait_send()
-    for c in second:
-        c.wait()
+    for k, c in enumerate(second):
+        c.wait_send()
+        if k >= 2:
+            c.wait_recv()
 
 
 def relayout(x, dest, count):
@@ -344,9 +346,10 @@
     return pl.pallas_call(
         relayout_kernel,
         out_shape=jax.ShapeDtypeStruct((704, 512), f32),
-        in_specs=[vm] * 3, out_specs=vm,
-        scratch_shapes=[pltpu.VMEM((5, 64, 640), f32)] * 2 + [pltpu.VMEM((3, 256, 512), bf16)]
-        + [pltpu.SemaphoreType.DMA((5,))] * 2 + [pltpu.SemaphoreType.DMA((6,))] * 2,
+        in_specs=[pl.BlockSpec(memory_space=pl.ANY), vm, vm], out_specs=vm,
+        scratch_shapes=[pltpu.VMEM((1024, 128), f32)] + [pltpu.VMEM((5, 72, 512), f32)] * 2
+        + [pltpu.VMEM((3, 256, 512), bf16)]
+        + [pltpu.SemaphoreType.DMA((5,))] * 2 + [pltpu.SemaphoreType.DMA((7,))] * 2 + [pltpu.SemaphoreType.DMA],
         compiler_params=pltpu.CompilerParams(collective_id=0, has_side_effects=True, vmem_limit_bytes=32 * 2**20),
         name="relayout",
     )(x, dest, count)
@@ -355,17 +358,16 @@
 BACK = ((320, 64, (1, 1)), (384, 64, (1, -1)), (192, 128, (1, 0)), (0, 128, (0, 1)), (128, 64, (0, -1)))
 
 
-def combine_kernel(sums, cells, cnt_ref, dens, lap, got, field, s1, r1, fsem):
+def combine_kernel(sums, cells, dens, lap, got, own_cells, s1, r1, fsem):
     greet([(0, -1), (0, 1), (-1, 0), (-1, -1), (-1, 1)])
-    fetch = pltpu.make_async_copy(cells.at[pl.ds(0, 256), pl.ds(384, 128)], field, fsem)
+    fetch = pltpu.make_async_copy(cells.at[pl.ds(0, 256)], own_cells, fsem)
     fetch.start()
     copies = []
     for k, (row, rows, where) in enumerate(BACK):
         c = copy_to(sums.at[:, pl.ds(256 + row, rows)], got.at[:, pl.ds(row, rows)], s1.at[k], r1.at[k], where)
         c.start()
         copies.append(c)
-    diag = jnp.where(iota((256, 256), 0) == iota((256, 256), 1), 1.0, 0.0)
-    count = jnp.sum(diag * cnt_ref[...].astype(f32), axis=1, keepdims=True)
+    x0, _ = centre()
     fetch.wait()
     for c in copies:
         c.wait()
@@ -378,31 +380,28 @@
         for r in lists[q]:
             n = n + got[0, r:r + 64, :]
             s = s + got[1, r:r + 64, :]
-        filled = iota((64, 128), 1) < count[rows]
+        filled = own_cells[rows, 0:128] - x0 < 0.5 * SENT
         dens[rows, :] = jnp.where(filled, (n - own) / ref_density, 0.0)
-        lap[rows, :] = jnp.where(filled, (s - field[rows, :] * n) / ref_density, 0.0)
-
-
-def combine(sums, cells, count):
+        lap[rows, :] = jnp.where(filled, (s - own_cells[rows, 384:512] * n) / ref_density, 0.0)
+
+
+def combine(sums, cells):
     vm = pl.BlockSpec(memory_space=pltpu.VMEM)
     return pl.pallas_call(
         combine_kernel,
         out_shape=[jax.ShapeDtypeStruct((256, 128), f32)] * 2,
-        in_specs=[vm, pl.BlockSpec(memory_space=pl.ANY), vm], out_specs=[vm] * 2,
-        scratch_shapes=[pltpu.VMEM((2, 448, 128), f32), pltpu.VMEM((256, 128), f32), pltpu.SemaphoreType.DMA((5,)), pltpu.SemaphoreType.DMA((5,)),
+        in_specs=[vm, pl.BlockSpec(memory_space=pl.ANY)], out_specs=[vm] * 2,
+        scratch_shapes=[pltpu.VMEM((2, 448, 128), f32), pltpu.VMEM((256, 512), f32), pltpu.SemaphoreType.DMA((5,)), pltpu.SemaphoreType.DMA((5,)),
                         pltpu.SemaphoreType.DMA],
         compiler_params=pltpu.CompilerParams(collective_id=1, has_side_effects=True, vmem_limit_bytes=16 * 2**20),
         name="combine",
-    )(sums, cells, count)
+    )(sums, cells)
 
 
 def local(incoming, dest, counts):
-    count = counts.reshape(256)
-    x0 = (lax.axis_index("slab") * 2 + 1).astype(f32)
-    y0 = (lax.axis_index("dom") * 2 + 1).astype(f32)
-    cells = relayout(incoming.reshape(256, 4, 128), dest, count.reshape(1, 256))
-    sums = compute(jnp.stack([x0, y0]), count, cells)
-    density, laplace = combine(sums, cells, count.reshape(1, 256))
+    cells = relayout(incoming.reshape(1024, 128), dest, counts)
+    sums = compute(counts, cells)
+    density, laplace = combine(sums, cells)
     return density.reshape(2, 2, 64, 128), laplace.reshape(2, 2, 64, 128)
 
 

time: 156 us -> 153 us (0.981)
  local copies, waits for them, and re-layouts: 8.7 us -> 3.71 us
  Pallas kernels: 145 us -> 148 us
    pallas_call x1, Pallas kernels: 106 us -> 110 us  [compute(): pl.pallas_call(kern, out_shape=jax.ShapeDtypeStruct((2, 704, 128), f32),...]
    pallas_call x1, Pallas kernels: 27 us -> 23.6 us  [relayout(): pl.pallas_call(relayout_kernel, out_shape=jax.ShapeDtypeStruct((704, 512)...]
    pallas_call x1, Pallas kernels: 12.1 us -> 15.2 us  [combine(): pl.pallas_call(combine_kernel, out_shape=[jax.ShapeDtypeStruct((256, 128)...]
    unnamed x12 -> x8, local copies, waits for them, and re-layouts: 6.62 us -> 3.71 us
where the time goes in v4:
time: 153 us
  Pallas kernels  148 us (97%)
  local copies, waits for them, and re-layouts  3.71 us (2%)
    pallas_call x1, Pallas kernels, compute(): pl.pallas_call(kern, out_shape=jax.ShapeDtypeStruct((2, 704, 128), f32),...  110 us
    pallas_call x1, Pallas kernels, relayout(): pl.pallas_call(relayout_kernel, out_shape=jax.ShapeDtypeStruct((704, 512)...  23.6 us
    pallas_call x1, Pallas kernels, combine(): pl.pallas_call(combine_kernel, out_shape=[jax.ShapeDtypeStruct((256, 128)...  15.2 us
    unnamed x8, local copies, waits for them, and re-layouts  3.71 us

profile of v4, /device:TPU:1, one launch (start us, length us, event | category | flops | bytes accessed | tf_op | source)
XLA Modules:
  0.0 152.7 jit_solution(11677663378018171670)
XLA Ops:
  0.6 0.0 copy-start
  0.6 1.0 copy-done
  1.7 0.0 copy-start.1
  1.7 0.7 copy-done.1
  2.4 0.0 copy-start.2
  2.4 0.7 copy-done.2
  3.0 23.6 %relayout.1.cells = f32[704,512]{1,0:T(8,128)S(1)} custom-call(f32[1024,128]{1,0:T(8,128)S(1)} %bitcast.3, s32[1,256]{1,0:T(1,128)S(1)} %copy-done.2, s32[2,2,64]{2,1,0:T(2,128)S(1)} %copy-done.1), custom_call_target="tpu_custom_call" | custom-call | tf_op jit(solution)/shard_map/relayout/pallas_call | solution.py:346
  26.7 109.5 %pairs.1.sums = f32[2,704,128]{2,1,0:T(8,128)S(1)} custom-call(s32[2,2,64]{2,1,0:T(2,128)S(1)} %copy-done.1, f32[704,512]{1,0:T(8,128)S(1)} %relayout.1.cells), custom_call_target="tpu_custom_call" | custom-call | tf_op jit(solution)/shard_map/pairs/pallas_call | solution.py:233
  136.2 15.2 %combine.1 = (f32[256,128]{1,0:T(8,128)S(1)}, f32[256,128]{1,0:T(8,128)S(1)}) custom-call(f32[2,704,128]{2,1,0:T(8,128)S(1)} %pairs.1.sums, f32[704,512]{1,0:T(8,128)S(1)} %relayout.1.cells), custom_call_target="tpu_custom_call" | custom-call | tf_op jit(solution)/shard_map/combine/pallas_call | solution.py:390
  151.4 0.7 copy.7
  152.1 0.7 copy.8
Async XLA Ops:
  0.6 1.0 copy-start
  1.7 0.7 copy-start.1
  2.4 0.7 copy-start.2

commit v5 on v4

--- a/solution.py
+++ b/solution.py
@@ -37,7 +37,7 @@
     return [h, m, h, m]
 
 
-def build_cols(p_ref, row0, col, x0, y0, own_cell, b_ref, f_ref, a_ref, stage, stage_a):
+def build_cols(p_ref, row0, col, x0, y0, own_cell, b_ref, f_ref, stage, stage_a):
     @pl.loop(0, 8)
     def _(k):
         z0 = k * 8
@@ -62,25 +62,35 @@
             terms.update(enumerate(left(h, m) + list(split3(xy + zs * zs)), 16 + 16 * k2))
         terms.update(enumerate(split3(f), 23))
         for r, v in terms.items():
-            stage_a[pl.ds(r, 8, stride=64), :] = v
-        for j in range(8):
-            t = stage_a[j * 64:j * 64 + 64, :].T
-            a_ref[pl.ds(pl.multiple_of((own_cell + z0 + j) * 128, 128), 128), :] = t.astype(bf16)
+            stage_a[pl.ds((own_cell + z0) * 64 + r, 8, stride=64), :] = v
 
 
 def cell_of(cell):
-    cx, cy, z = cell // 128, (cell // 64) % 2, cell % 64
-    return [((cx + dx) * 4 + cy + 1 + dy) * ZP + 1 + z + dz for dx, dy, dz in OFFS]
+    cell = jnp.asarray(cell, jnp.int32)
+    cx, cy, z = cell >> 7, (cell >> 6) & 1, cell & 63
+    return (cx * 4 + cy + 1) * ZP + 1 + z
+
+
+STEPS = [(dx * 4 + dy) * ZP + dz for dx, dy, dz in OFFS]
+
+
+def rows_of(base, count):
+    first = base * count
+    return [pl.ds(pl.multiple_of(first + step * count, count), count) for step in STEPS]
+
+
+def turn(cell, a_ref, stage_a):
+    a_ref[...] = stage_a[pl.ds(pl.multiple_of(cell * 64, 64), 64), :].T.astype(bf16)
 
 
 def make_d(cell, d_ref, a_ref, b_ref):
-    a = a_ref[pl.ds(pl.multiple_of(cell * 128, 128), 128), :]
+    a = a_ref[...]
     zero = jnp.zeros((16, 128), bf16)
     ri = lax.broadcasted_iota(jnp.int32, (16, 128), 0)
     pick = jnp.where((ri >= 7) & (ri < 10), 1.0, 0.0).astype(bf16)
     ws = []
-    for (dx, dy, dz), c in zip(OFFS, cell_of(cell)):
-        b = b_ref[pl.ds(pl.multiple_of(c * 32, 32), 32), :]
+    for (dx, dy, dz), rows in zip(OFFS, rows_of(cell_of(cell), 32)):
+        b = b_ref[rows, :]
         ws.append(jnp.concatenate([b[:16]] + [b[16:] if k == dz else zero for k in (-1, 0, 1)], 0))
     ws.append(jnp.concatenate([zero, pick, zero, zero], 0))
 
@@ -100,16 +110,16 @@
         for part in parts:
             part()
         return
-    cs = cell_of(cell)
-    fj = [jnp.broadcast_to(f_ref[pl.ds(c, 1), :], (8, 128)) for c in cs]
+    base = cell_of(cell)
+    fj = [jnp.broadcast_to(f_ref[pl.ds(base + step, 1), :], (8, 128)) for step in STEPS]
     f0 = fj[0]
     for v in fj[1:]:
         f0 = f0 + v
-    cn = [jnp.full((8, 128), -(R // 8.0), f32) for _ in cs]
+    cn = [jnp.full((8, 128), -(R // 8.0), f32) for _ in STEPS]
     fi0 = d_ref[0:8, 128 * NT:128 * NT + 128]
     for r in range(8, R, 8):
         fi0 = fi0 + d_ref[r:r + 8, 128 * NT:128 * NT + 128]
-    cm = [-fi0 for _ in cs]
+    cm = [-fi0 for _ in STEPS]
     for r in range(0, R, 8):
         fi = d_ref[r:r + 8, 128 * NT:128 * NT + 128]
         an = jnp.full((8, 128), -float(NT), f32)
@@ -126,7 +136,7 @@
         as_ref[r:r + 8, :] = am
         for part in parts[min(FR * r * len(parts) // R // 4, len(parts)):min(FR * (r + 8) * len(parts) // R // 4, len(parts))]:
             part()
-    rows = [pl.ds(pl.multiple_of(c * 8, 8), 8) for c in cs]
+    rows = rows_of(base, 8)
     olds = [(jn_ref[rows[t], :], js_ref[rows[t], :]) for t in range(1, NT)]
     for t in range(1, NT):
         jn_ref[rows[t], :] = olds[t - 1][0] + cn[t]
@@ -153,10 +163,14 @@
 
 
 def kern(cnt_ref, cells, out_ref,
-         a_ref, b_ref, f_ref, jn_ref, js_ref, stage, stage_a, d0, d1, an0, as0, an1, as1):
+         a0, a1, b_ref, f_ref, jn_ref, js_ref, stage, stage_a, d0, d1, an0, as0, an1, as1):
     x0, y0 = centre()
-    ra = lax.broadcasted_iota(jnp.int32, stage_a.shape, 0) % 64
-    stage_a[...] = jnp.where((ra >= 8) & (ra < 11), 1.0, 0.0)
+    ra = lax.broadcasted_iota(jnp.int32, (64, 128), 0)
+    ones = jnp.where((ra >= 8) & (ra < 11), 1.0, 0.0)
+
+    @pl.loop(0, 256)
+    def _(k):
+        stage_a[pl.ds(pl.multiple_of(k * 64, 64), 64), :] = ones
     rb = lax.broadcasted_iota(jnp.int32, stage.shape, 0) % 32
     stage[...] = jnp.where((rb >= 20) & (rb < 23), 1.0, 0.0)
     ri = lax.broadcasted_iota(jnp.int32, (32, 128), 0)
@@ -174,7 +188,7 @@
         jn_ref[rows, :] = jnp.zeros((8 * ZP, 128), f32)
         js_ref[rows, :] = jnp.zeros((8 * ZP, 128), f32)
 
-    b = functools.partial(build_cols, x0=x0, y0=y0, b_ref=b_ref, f_ref=f_ref, a_ref=a_ref, stage=stage, stage_a=stage_a)
+    b = functools.partial(build_cols, x0=x0, y0=y0, b_ref=b_ref, f_ref=f_ref, stage=stage, stage_a=stage_a)
 
     @pl.loop(0, 4)
     def _(k):
@@ -185,9 +199,11 @@
         col = jnp.where(k < 2, 3 + 4 * k, jnp.where(k < 3, 4, jnp.where(k < 6, 6 + k, 8)))
         b(cells, 256 + k * 64, col, own_cell=None)
 
-    for part in make_d(0, d0, a_ref, b_ref):
+    turn(0, a0, stage_a)
+    turn(1, a1, stage_a)
+    for part in make_d(0, d0, a0, b_ref):
         part()
-    bufs = ((d0, an0, as0), (d1, an1, as1))
+    bufs = ((d0, an0, as0, a0), (d1, an1, as1, a1))
 
     @pl.loop(0, 128)
     def _(i):
@@ -195,14 +211,16 @@
             cell = i * 2 + p
             nxt = jnp.minimum(cell + 1, 255)
             prev = jnp.maximum(cell - 1, 0)
-            d, an, am = bufs[p]
-            dn, anp, amp = bufs[1 - p]
+            d, an, am, a = bufs[p]
+            dn, anp, amp, a_next = bufs[1 - p]
+            later = jnp.minimum(cell + 2, 255)
 
             def run(k):
-                parts = make_d(nxt, dn, a_ref, b_ref)
+                turn(later, a, stage_a)
+                parts = make_d(nxt, dn, a_next, b_ref)
                 finish(prev, anp, amp, out_ref)
                 pair_sums(16 * k, cell, d, an, am, f_ref, jn_ref, js_ref, parts)
-            tree((cnt_ref[cell // 128, (cell // 64) % 2, cell % 64] + 15) // 16, 0, 9, run)
+            tree((cnt_ref[cell >> 7, (cell >> 6) & 1, cell & 63] + 15) >> 4, 0, 9, run)
     finish(255, an1, as1, out_ref)
 
     def side(col, z0, ref):
@@ -234,9 +252,9 @@
         kern,
         out_shape=jax.ShapeDtypeStruct((2, 704, 128), f32),
         in_specs=[sm, vm], out_specs=vm,
-        scratch_shapes=[pltpu.VMEM((256 * 128, 64), bf16), pltpu.VMEM((12 * ZP * 32, 128), bf16),
+        scratch_shapes=[pltpu.VMEM((128, 64), bf16), pltpu.VMEM((128, 64), bf16), pltpu.VMEM((12 * ZP * 32, 128), bf16),
                         pltpu.VMEM((12 * ZP, 128), f32), pltpu.VMEM((12 * ZP * 8, 128), f32), pltpu.VMEM((12 * ZP * 8, 128), f32),
-                        pltpu.VMEM((256, 128), f32), pltpu.VMEM((512, 128), f32)]
+                        pltpu.VMEM((256, 128), f32), pltpu.VMEM((256 * 64, 128), f32)]
         + [pltpu.VMEM((128, 128 * (NT + 1)), f32)] * 2 + [pltpu.VMEM((128, 128), f32)] * 4,
         compiler_params=pltpu.CompilerParams(vmem_limit_bytes=30 * 2**20),
         name="pairs",

time: 153 us -> 142 us (0.928)
  Pallas kernels: 148 us -> 138 us
    pallas_call x1, Pallas kernels: 110 us -> 98.9 us  [compute(): pl.pallas_call(kern, out_shape=jax.ShapeDtypeStruct((2, 704, 128), f32),...]
where the time goes in v5:
time: 142 us
  Pallas kernels  138 us (97%)
  local copies, waits for them, and re-layouts  3.71 us (3%)
    pallas_call x1, Pallas kernels, compute(): pl.pallas_call(kern, out_shape=jax.ShapeDtypeStruct((2, 704, 128), f32),...  98.9 us
    pallas_call x1, Pallas kernels, relayout(): pl.pallas_call(relayout_kernel, out_shape=jax.ShapeDtypeStruct((704, 512)...  23.6 us
    pallas_call x1, Pallas kernels, combine(): pl.pallas_call(combine_kernel, out_shape=[jax.ShapeDtypeStruct((256, 128)...  15.1 us
    unnamed x8, local copies, waits for them, and re-layouts  3.71 us

profile of v5, /device:TPU:1, one launch (start us, length us, event | category | flops | bytes accessed | tf_op | source)
XLA Modules:
  0.0 142.0 jit_solution(3218253564496389637)
XLA Ops:
  0.6 0.0 copy-start
  0.6 1.0 copy-done
  1.7 0.0 copy-start.1
  1.7 0.7 copy-done.1
  2.4 0.0 copy-start.2
  2.4 0.7 copy-done.2
  3.0 23.6 %relayout.1.cells = f32[704,512]{1,0:T(8,128)S(1)} custom-call(f32[1024,128]{1,0:T(8,128)S(1)} %bitcast.3, s32[1,256]{1,0:T(1,128)S(1)} %copy-done.2, s32[2,2,64]{2,1,0:T(2,128)S(1)} %copy-done.1), custom_call_target="tpu_custom_call" | custom-call | tf_op jit(solution)/shard_map/relayout/pallas_call | solution.py:364
  26.7 98.9 %pairs.1.sums = f32[2,704,128]{2,1,0:T(8,128)S(1)} custom-call(s32[2,2,64]{2,1,0:T(2,128)S(1)} %copy-done.1, f32[704,512]{1,0:T(8,128)S(1)} %relayout.1.cells), custom_call_target="tpu_custom_call" | custom-call | tf_op jit(solution)/shard_map/pairs/pallas_call | solution.py:251
  125.6 15.1 %combine.1 = (f32[256,128]{1,0:T(8,128)S(1)}, f32[256,128]{1,0:T(8,128)S(1)}) custom-call(f32[2,704,128]{2,1,0:T(8,128)S(1)} %pairs.1.sums, f32[704,512]{1,0:T(8,128)S(1)} %relayout.1.cells), custom_call_target="tpu_custom_call" | custom-call | tf_op jit(solution)/shard_map/combine/pallas_call | solution.py:408
  140.7 0.7 copy.7
  141.3 0.7 copy.8
Async XLA Ops:
  0.6 1.0 copy-start
  1.7 0.7 copy-start.1
  2.4 0.7 copy-start.2

commit v6 on v5

--- a/solution.py
+++ b/solution.py
@@ -168,9 +168,10 @@
     ra = lax.broadcasted_iota(jnp.int32, (64, 128), 0)
     ones = jnp.where((ra >= 8) & (ra < 11), 1.0, 0.0)
 
-    @pl.loop(0, 256)
-    def _(k):
-        stage_a[pl.ds(pl.multiple_of(k * 64, 64), 64), :] = ones
+    @pl.loop(0, 32)
+    def _(k):
+        for j in range(8):
+            stage_a[pl.ds(pl.multiple_of(k * 512 + 64 * j, 64), 64), :] = ones
     rb = lax.broadcasted_iota(jnp.int32, stage.shape, 0) % 32
     stage[...] = jnp.where((rb >= 20) & (rb < 23), 1.0, 0.0)
     ri = lax.broadcasted_iota(jnp.int32, (32, 128), 0)

time: 142 us -> 141 us (level)
  no operation moved by 1% of the time
where the time goes in v6:
time: 141 us
  Pallas kernels  137 us (97%)
  local copies, waits for them, and re-layouts  3.71 us (3%)
    pallas_call x1, Pallas kernels, compute(): pl.pallas_call(kern, out_shape=jax.ShapeDtypeStruct((2, 704, 128), f32),...  98.3 us
    pallas_call x1, Pallas kernels, relayout(): pl.pallas_call(relayout_kernel, out_shape=jax.ShapeDtypeStruct((704, 512)...  23.6 us
    pallas_call x1, Pallas kernels, combine(): pl.pallas_call(combine_kernel, out_shape=[jax.ShapeDtypeStruct((256, 128)...  15.1 us
    unnamed x8, local copies, waits for them, and re-layouts  3.71 us

profile of v6, /device:TPU:1, one launch (start us, length us, event | category | flops | bytes accessed | tf_op | source)
XLA Modules:
  0.0 141.5 jit_solution(8432213547015943394)
XLA Ops:
  0.6 0.0 copy-start
  0.6 1.0 copy-done
  1.7 0.0 copy-start.1
  1.7 0.7 copy-done.1
  2.4 0.0 copy-start.2
  2.4 0.7 copy-done.2
  3.0 23.6 %relayout.1.cells = f32[704,512]{1,0:T(8,128)S(1)} custom-call(f32[1024,128]{1,0:T(8,128)S(1)} %bitcast.3, s32[1,256]{1,0:T(1,128)S(1)} %copy-done.2, s32[2,2,64]{2,1,0:T(2,128)S(1)} %copy-done.1), custom_call_target="tpu_custom_call" | custom-call | tf_op jit(solution)/shard_map/relayout/pallas_call | solution.py:365
  26.7 98.3 %pairs.1.sums = f32[2,704,128]{2,1,0:T(8,128)S(1)} custom-call(s32[2,2,64]{2,1,0:T(2,128)S(1)} %copy-done.1, f32[704,512]{1,0:T(8,128)S(1)} %relayout.1.cells), custom_call_target="tpu_custom_call" | custom-call | tf_op jit(solution)/shard_map/pairs/pallas_call | solution.py:252
  125.0 15.1 %combine.1 = (f32[256,128]{1,0:T(8,128)S(1)}, f32[256,128]{1,0:T(8,128)S(1)}) custom-call(f32[2,704,128]{2,1,0:T(8,128)S(1)} %pairs.1.sums, f32[704,512]{1,0:T(8,128)S(1)} %relayout.1.cells), custom_call_target="tpu_custom_call" | custom-call | tf_op jit(solution)/shard_map/combine/pallas_call | solution.py:409
  140.1 0.7 copy.7
  140.8 0.7 copy.8
Async XLA Ops:
  0.6 1.0 copy-start
  1.7 0.7 copy-start.1
  2.4 0.7 copy-start.2

commit v7 on v6

--- a/solution.py
+++ b/solution.py
@@ -369,7 +369,7 @@
         scratch_shapes=[pltpu.VMEM((1024, 128), f32)] + [pltpu.VMEM((5, 72, 512), f32)] * 2
         + [pltpu.VMEM((3, 256, 512), bf16)]
         + [pltpu.SemaphoreType.DMA((5,))] * 2 + [pltpu.SemaphoreType.DMA((7,))] * 2 + [pltpu.SemaphoreType.DMA],
-        compiler_params=pltpu.CompilerParams(collective_id=0, has_side_effects=True, vmem_limit_bytes=32 * 2**20),
+        compiler_params=pltpu.CompilerParams(collective_id=0, has_side_effects=True, vmem_limit_bytes=56 * 2**20),
         name="relayout",
     )(x, dest, count)
 

time: 141 us -> 142 us (level)
  Pallas kernels: 137 us -> 139 us
    pallas_call x1, Pallas kernels: 23.6 us -> 25.5 us  [relayout(): pl.pallas_call(relayout_kernel, out_shape=jax.ShapeDtypeStruct((704, 512)...]
    unnamed x8 -> x6, local copies, waits for them, and re-layouts: 3.71 us -> 2.67 us
where the time goes in v7:
time: 142 us
  Pallas kernels  139 us (98%)
  local copies, waits for them, and re-layouts  2.67 us (2%)
    pallas_call x1, Pallas kernels, compute(): pl.pallas_call(kern, out_shape=jax.ShapeDtypeStruct((2, 704, 128), f32),...  98.5 us
    pallas_call x1, Pallas kernels, relayout(): pl.pallas_call(relayout_kernel, out_shape=jax.ShapeDtypeStruct((704, 512)...  25.5 us
    pallas_call x1, Pallas kernels, combine(): pl.pallas_call(combine_kernel, out_shape=[jax.ShapeDtypeStruct((256, 128)...  15 us

profile of v7, /device:TPU:1, one launch (start us, length us, event | category | flops | bytes accessed | tf_op | source)
XLA Modules:
  0.0 142.3 jit_solution(1476335050007928799)
XLA Ops:
  0.6 0.0 copy-start.1
  0.6 25.5 %relayout.1.cells = f32[704,512]{1,0:T(8,128)} custom-call(f32[1024,128]{1,0:T(8,128)} %bitcast.5, s32[1,256]{1,0:T(1,128)} %dest_ref.1, s32[2,2,64]{2,1,0:T(2,128)} %cnt_ref.3), custom_call_target="tpu_custom_call" | custom-call | tf_op jit(solution)/shard_map/relayout/pallas_call | solution.py:365
  26.1 0.0 copy-done.1
  26.1 0.0 copy-start
  26.1 1.4 copy-done
  27.5 98.5 %pairs.1.sums = f32[2,704,128]{2,1,0:T(8,128)S(1)} custom-call(s32[2,2,64]{2,1,0:T(2,128)S(1)} %copy-done.1, f32[704,512]{1,0:T(8,128)S(1)} %copy-done), custom_call_target="tpu_custom_call" | custom-call | tf_op jit(solution)/shard_map/pairs/pallas_call | solution.py:252
  126.0 15.0 %combine.1 = (f32[256,128]{1,0:T(8,128)S(1)}, f32[256,128]{1,0:T(8,128)S(1)}) custom-call(f32[2,704,128]{2,1,0:T(8,128)S(1)} %pairs.1.sums, f32[704,512]{1,0:T(8,128)S(1)} %copy-done), custom_call_target="tpu_custom_call" | custom-call | tf_op jit(solution)/shard_map/combine/pallas_call | solution.py:409
  141.0 0.7 copy.7
  141.6 0.7 copy.8
Async XLA Ops:
  0.6 25.5 %copy-start.1 = (s32[2,2,64]{2,1,0:T(2,128)S(1)}, s32[2,2,64]{2,1,0:T(2,128)}, u32[]{:S(2)}) copy-start(s32[2,2,64]{2,1,0:T(2,128)} %cnt_ref.3) | copy-start | bytes 3076
  26.1 1.4 copy-start

commit v8 on v6

--- a/solution.py
+++ b/solution.py
@@ -339,19 +339,23 @@
     for c in first:
         c.wait_recv()
     label = jnp.concatenate([got[k, 64:65, 0:64] for k in range(5)], 1)
-    place = jnp.where(iota((256, 320), 0) + 1.0 == label, 1.0, 0.0).astype(bf16)
-    total = picked(place, jnp.concatenate([got[k, 0:64, :] for k in range(5)], 0), ((1,), (0,)))
+    data = jnp.concatenate([got[k, 0:64, :] for k in range(5)], 0)
     x0, _ = centre()
-    cells[0:256, 0:128] = jnp.where(filled, total[:, 0:128], x0 + SENT)
-    cells[0:256, 128:384] = total[:, 128:384]
-    cells[0:256, 384:512] = jnp.where(filled, total[:, 384:512], 0.0)
     second = []
-    for k, (row, rows, where, there) in enumerate(HALO):
-        if k >= 5:
-            second[k - 5].wait_recv()
-        c = copy_to(cells.at[pl.ds(row, rows)], cells.at[pl.ds(there, rows)], s2.at[k], r2.at[k], where)
-        c.start()
-        second.append(c)
+    for half in range(2):
+        a, b = 128 * half, 128 * half + 128
+        place = jnp.where(iota((128, 320), 0) + (1.0 + a) == label, 1.0, 0.0).astype(bf16)
+        total = picked(place, data, ((1,), (0,)))
+        cells[a:b, 0:128] = jnp.where(filled[a:b], total[:, 0:128], x0 + SENT)
+        cells[a:b, 128:384] = total[:, 128:384]
+        cells[a:b, 384:512] = jnp.where(filled[a:b], total[:, 384:512], 0.0)
+        for k in ((0, 1, 2) if half == 0 else (3, 4, 5, 6)):
+            row, rows, where, there = HALO[k]
+            if k >= 5:
+                second[k - 5].wait_recv()
+            c = copy_to(cells.at[pl.ds(row, rows)], cells.at[pl.ds(there, rows)], s2.at[k], r2.at[k], where)
+            c.start()
+            second.append(c)
     for c in first:
         c.wait_send()
     for k, c in enumerate(second):

time: 141 us -> 141 us (level)
  no operation moved by 1% of the time
where the time goes in v8:
time: 141 us
  Pallas kernels  136 us (96%)
  local copies, waits for them, and re-layouts  3.71 us (3%)
    pallas_call x1, Pallas kernels, compute(): pl.pallas_call(kern, out_shape=jax.ShapeDtypeStruct((2, 704, 128), f32),...  98.1 us
    pallas_call x1, Pallas kernels, relayout(): pl.pallas_call(relayout_kernel, out_shape=jax.ShapeDtypeStruct((704, 512)...  23.5 us
    pallas_call x1, Pallas kernels, combine(): pl.pallas_call(combine_kernel, out_shape=[jax.ShapeDtypeStruct((256, 128)...  14.9 us
    unnamed x8, local copies, waits for them, and re-layouts  3.71 us

profile of v8, /device:TPU:1, one launch (start us, length us, event | category | flops | bytes accessed | tf_op | source)
XLA Modules:
  0.0 140.8 jit_solution(15512953960960160213)
XLA Ops:
  0.6 0.0 copy-start
  0.6 1.0 copy-done
  1.7 0.0 copy-start.1
  1.7 0.7 copy-done.1
  2.4 0.0 copy-start.2
  2.4 0.7 copy-done.2
  3.0 23.5 %relayout.1.cells = f32[704,512]{1,0:T(8,128)S(1)} custom-call(f32[1024,128]{1,0:T(8,128)S(1)} %bitcast.3, s32[1,256]{1,0:T(1,128)S(1)} %copy-done.2, s32[2,2,64]{2,1,0:T(2,128)S(1)} %copy-done.1), custom_call_target="tpu_custom_call" | custom-call | tf_op jit(solution)/shard_map/relayout/pallas_call | solution.py:369
  26.5 98.1 %pairs.1.sums = f32[2,704,128]{2,1,0:T(8,128)S(1)} custom-call(s32[2,2,64]{2,1,0:T(2,128)S(1)} %copy-done.1, f32[704,512]{1,0:T(8,128)S(1)} %relayout.1.cells), custom_call_target="tpu_custom_call" | custom-call | tf_op jit(solution)/shard_map/pairs/pallas_call | solution.py:252
  124.6 14.9 %combine.1 = (f32[256,128]{1,0:T(8,128)S(1)}, f32[256,128]{1,0:T(8,128)S(1)}) custom-call(f32[2,704,128]{2,1,0:T(8,128)S(1)} %pairs.1.sums, f32[704,512]{1,0:T(8,128)S(1)} %relayout.1.cells), custom_call_target="tpu_custom_call" | custom-call | tf_op jit(solution)/shard_map/combine/pallas_call | solution.py:413
  139.5 0.7 copy.7
  140.2 0.7 copy.8
Async XLA Ops:
  0.6 1.0 copy-start
  1.7 0.7 copy-start.1
  2.4 0.7 copy-start.2
